TPU v7x, 128 devices: a whole 4x4x4 slice. The times are simulated.
128 devices in a mesh: grp: 8 (over x, core), tile: 16 (over y, z).
Axes of the slice: x: 4, y: 4, z: 4, core: 2. Of those that a mesh axis runs over, the one named last changes fastest.
Arguments:
- molecule_coords: float32 [3, 2097152], P(None, ('grp', 'tile')), may hold values from 0 to 1.6
- molecule_speeds: float32 [3, 2097152], P(None, ('grp', 'tile')), may hold values from -6 to 6
- molecule_thermal_state: float32 [2097152], P(('grp', 'tile')), may hold values from 0.5 to 2
- conservative_strength: float32 [2097152], P(('grp', 'tile')), may hold values from 0.05 to 0.5
- noise_keys: int32 [2097152], P(('grp', 'tile')), may hold values from 0 to 32767
- exported_tile_places: int32 [128, 16, 12], P(('grp', 'tile')), may hold values from 0 to 127
- tile_couplings: int32 [128, 1024, 2], P(('grp', 'tile')), may hold values from 0 to 383, as said below
- processor_coupling_tally: int32 [128], P(('grp', 'tile')), may hold values from 512 to 1024
Outputs:
- force_heat: float32 [4, 2097152], P(None, ('grp', 'tile'))
Inputs may be any that keep to these rules, and one draw needn't show every extreme that they name: `tile_couplings`: second slots of workers in the lowest slab are below 192; first slots are below 192.
All inputs are finite; a program needn't handle non-finite values.
Results may differ from a plain program's by a relative error of at most 0.0003.
Values sent between devices are 32-bit elements; how exact they have to be, the bound alone decides.
A program may use at most 128 MiB of HBM per device.

v0:
```python
import math

import jax
import jax.numpy as jnp
from jax import lax
from jax.sharding import PartitionSpec as P

friction = 0.45
noise_amp = 0.3
conductivity = 0.1


def passed_along(value, axis, steps):
    count = lax.axis_size(axis)
    leading, last = (max(0, -steps), min(count, count - steps))
    return lax.ppermute(value, axis, [(source, source + steps) for source in range(leading, last)])


def tile_pair(first, second):
    offset = first[0:3, :, None] - second[0:3, None, :]
    radius = jnp.sqrt(jnp.sum(offset * offset, 0) + 0.01)
    unit = offset / radius
    weight = jnp.maximum(1.0 - radius, 0.0)
    relative = first[3:6, :, None] - second[3:6, None, :]
    along = jnp.sum(unit * relative, 0)
    repulse = 0.5 * (first[7][:, None] + second[7][None, :])
    seed_first = first[8].astype(jnp.int32)
    seed_second = second[8].astype(jnp.int32)
    hashed = (
        seed_first[:, None] * seed_second[None, :] + seed_first[:, None] + seed_second[None, :]
    ) % 65521
    noise = hashed.astype(jnp.float32) * (2.0 / 65521.0) - 1.0
    magnitude = repulse * weight - friction * weight * weight * along + noise_amp * weight * noise
    force = magnitude[None] * unit
    conduct = conductivity * weight * weight * (second[6][None, :] - first[6][:, None])
    viscous = 0.5 * friction * weight * weight * along * along
    on_first = jnp.concatenate([jnp.sum(force, 2), jnp.sum(conduct + viscous, 1)[None]], 0)
    on_second = jnp.concatenate([-jnp.sum(force, 1), jnp.sum(viscous - conduct, 0)[None]], 0)
    return (on_first, on_second)


def tile_self(block_data):
    offset = block_data[0:3, :, None] - block_data[0:3, None, :]
    radius = jnp.sqrt(jnp.sum(offset * offset, 0) + 0.01)
    unit = offset / radius
    weight = jnp.maximum(1.0 - radius, 0.0)
    relative = block_data[3:6, :, None] - block_data[3:6, None, :]
    along = jnp.sum(unit * relative, 0)
    repulse = 0.5 * (block_data[7][:, None] + block_data[7][None, :])
    seed_first = block_data[8].astype(jnp.int32)
    hashed = (
        seed_first[:, None] * seed_first[None, :] + seed_first[:, None] + seed_first[None, :]
    ) % 65521
    noise = hashed.astype(jnp.float32) * (2.0 / 65521.0) - 1.0
    others = 1.0 - jnp.eye(block_data.shape[1], dtype=jnp.float32)
    magnitude = (
        repulse * weight - friction * weight * weight * along + noise_amp * weight * noise
    ) * others
    force = magnitude[None] * unit
    conduct = conductivity * weight * weight * (block_data[6][None, :] - block_data[6][:, None])
    viscous = 0.5 * friction * weight * weight * along * along
    heating = jnp.sum((conduct + viscous) * others, 1)
    return jnp.concatenate([jnp.sum(force, 2), heating[None]], 0)


def one_hot(indices, count):
    return (indices[:, None] == jnp.arange(count, dtype=jnp.int32)[None, :]).astype(jnp.float32)


def per_device(
    molecule_coords,
    molecule_speeds,
    molecule_thermal_state,
    conservative_strength,
    noise_keys,
    exported_tile_places,
    tile_couplings,
    processor_coupling_tally,
):
    n_tile = lax.axis_size("tile")
    blocks = molecule_coords.shape[1] // 128
    slot_table = exported_tile_places[0]
    cap = slot_table.shape[1]
    buffer_len = n_tile * cap
    owned = jnp.concatenate(
        [
            molecule_coords,
            molecule_speeds,
            molecule_thermal_state[None],
            conservative_strength[None],
            noise_keys[None].astype(jnp.float32),
        ],
        0,
    )
    owned = owned.reshape(9, blocks, 128).transpose(1, 0, 2)
    group_data = lax.all_gather(owned, "tile", axis=0, tiled=True)
    tables = lax.all_gather(exported_tile_places, "tile", axis=0, tiled=True)
    my_index = lax.axis_index("tile")
    my_slots = lax.dynamic_index_in_dim(tables, my_index, 1, keepdims=False)
    group_ids = (jnp.arange(n_tile, dtype=jnp.int32)[:, None] * blocks + my_slots).reshape(-1)
    held_blocks = group_data[group_ids]
    neighbour = passed_along(held_blocks, "grp", 1)
    reachable = jnp.concatenate([held_blocks, neighbour], 0)
    total_pair_count = tile_couplings.shape[1]
    batch = math.gcd(total_pair_count, 64)
    first_slots = tile_couplings[0, :, 0].reshape(-1, batch)
    second_slots = tile_couplings[0, :, 1].reshape(-1, batch)
    live_rows = (
        (jnp.arange(total_pair_count, dtype=jnp.int32) < processor_coupling_tally[0])
        .astype(jnp.float32)
        .reshape(-1, batch)
    )

    def consume(carry, items):
        near_acc, far_acc = carry
        first_idx, second_index, live = items
        on_first, on_second = jax.vmap(tile_pair)(held_blocks[first_idx], reachable[second_index])
        on_first = (on_first * live[:, None, None]).reshape(batch, 512)
        on_second = (on_second * live[:, None, None]).reshape(batch, 512)
        near_acc = near_acc + jnp.dot(
            one_hot(first_idx, buffer_len).T, on_first, precision=lax.Precision.HIGHEST
        )
        far_acc = far_acc + jnp.dot(
            one_hot(second_index, 2 * buffer_len).T, on_second, precision=lax.Precision.HIGHEST
        )
        return ((near_acc, far_acc), None)

    start_carry = (
        jnp.zeros((buffer_len, 512), jnp.float32),
        jnp.zeros((2 * buffer_len, 512), jnp.float32),
    )
    (near_acc, far_acc), _ = lax.scan(consume, start_carry, (first_slots, second_slots, live_rows))
    lower_terms = passed_along(far_acc[buffer_len:], "grp", -1)
    own_total = near_acc + far_acc[:buffer_len] + lower_terms
    selector = one_hot(group_ids, n_tile * blocks)
    summed = lax.psum_scatter(
        jnp.dot(selector.T, own_total, precision=lax.Precision.HIGHEST),
        "tile",
        scatter_dimension=0,
        tiled=True,
    )
    self_batch = math.gcd(blocks, 16)

    def self_step(carry, group_data):
        return (carry, jax.vmap(tile_self)(group_data))

    _, selfs = lax.scan(
        self_step, jnp.zeros((), jnp.float32), owned.reshape(-1, self_batch, 9, 128)
    )
    result = summed.reshape(blocks, 4, 128) + selfs.reshape(blocks, 4, 128)
    return result.transpose(1, 0, 2).reshape(4, blocks * 128)


def solution(mesh):
    in_specs = (
        P(None, ("grp", "tile")),
        P(None, ("grp", "tile")),
        P(("grp", "tile")),
        P(("grp", "tile")),
        P(("grp", "tile")),
        P(("grp", "tile"), None, None),
        P(("grp", "tile"), None, None),
        P(("grp", "tile")),
    )
    out_specs = P(None, ("grp", "tile"))
    return jax.shard_map(
        per_device, mesh=mesh, in_specs=in_specs, out_specs=out_specs, check_vma=False
    )
```

profile of v0, /device:TPU:99, one launch (start us, length us, event | category | flops | bytes accessed | tf_op | source)
XLA Modules:
  0.0 829.9 jit_solution(1761941762387604038)
XLA Ops:
  12.7 19.5 %all_gather.6 = s32[16,16,12]{2,1,0:T(8,128)S(1)} all-gather(s32[1,16,12]{2,1,0:T(8,128)S(1)} %copy.32), channel_id=1, replica_groups=mesh['grp'=8,'tile'=16] {'tile'}, dimensions={0}, use_global_device_ids=true | all-gather | bytes 13056 | tf_op jit(solution)/shard_map/all_gather | solution.py:97
  34.2 54.9 %all-gather.2.cloned.1.call-done = f32[2048,9,128]{2,0,1:T(8,128)} async-done(((f32[128,9,128]{2,0,1:T(8,128)}), f32[2048,9,128]{2,0,1:T(8,128)}) %all-gather.2.cloned.1.call-update) | async-done | bytes 9437200 | tf_op jit(solution)/shard_map/all_gather | solution.py:96
  89.1 12.8 %copy.33 = f32[2048,9,128]{2,1,0:T(8,128)} copy(f32[2048,9,128]{2,0,1:T(8,128)} %all-gather.2.cloned.1.call-done) | data formatting | bytes 18874368 | tf_op jit(solution)/shard_map/all_gather | solution.py:96
  101.8 6.5 gather_fusion.2
  114.6 8.8 %collective-permute-done = f32[192,9,128]{2,0,1:T(8,128)S(1)} collective-permute-done((f32[192,9,128]{2,0,1:T(8,128)}, f32[192,9,128]{2,0,1:T(8,128)S(1)}, u32[]{:S(2)}, u32[]{:S(2)}) %collective-permute-start) | collective-permute-done | bytes 884768 | tf_op jit(solution)/shard_map/ppermute | solution.py:16
  125.9 606.1 %while.28 = (s32[]{:T(128)}, f32[192,512]{1,0:T(8,128)}, f32[384,512]{1,0:T(8,128)S(1)}, s32[16,64]{1,0:T(8,128)S(1)}, f32[192,9,128]{2,1,0:T(8,128)S(1)}, /*ind...) while((s32[]{:T(128)}, f32[192,512]{1,0:T(8,128)}, ...), condition=%wide.region_7.8_spmd.clone, body=%wide.region_0.7_spmd.clone.sunk | while | flops 305871232 | bytes 52507452 | solution.py:132
  129.8 4.1 fusion.72
  135.1 8.0 multiply_reduce_fusion.11
  143.2 9.2 %subtract_reduce_fusion.2 = (f32[64,128]{1,0:T(8,128)S(1)}, f32[64,128]{1,0:T(8,128)S(1)}, f32[64,128,128]{2,1,0:T(8,128)S(1)}) fusion(f32[64,128,128]{2,1,0:T(8,128)S(1)} %multiply_reduce_fusion.11, f32[64,128]{1,0:T(8,128)S(1)} %bitcast.118, f32[64,128]{1,0:T(8,128)S(1)} %bitcast.115, f32[64,128,128]{2,1,0:T(8,128)S(1)} %fusion.72, ...), kind=kLoop, calls=%fused_computation.59.clone.1 | loop fusion | flops 38780928 | bytes 12845056 | tf_op jit(solution)/shard_map/while/body/eval_jaxpr/vmap()/reduce_sum | solution.py:38
  152.4 8.5 %multiply_reduce_fusion.12 = (f32[64,3,128]{2,1,0:T(4,128)S(1)}, f32[64,3,128]{2,1,0:T(4,128)S(1)}) fusion(f32[64,128,128]{2,1,0:T(8,128)S(1)} %get-tuple-element.365, f32[64,128,128]{2,1,0:T(8,128)S(1)} %add_sqrt_fusion.5, f32[64,3,128]{2,1,0:T(4,128)S(1)} %get-tuple-element.356, f32[64,3,128]{2,1,0:T(4,128)S(1)} %get-tuple-element.357), kind=kLoop, calls=%fused_computation.44.clone.1 | loop fusion | flops 15679488 | bytes 8781824 | tf_op jit(solution)/shard_map/while/body/eval_jaxpr/vmap()/reduce_sum | solution.py:38
  172.9 8.0 multiply_reduce_fusion.11
  181.1 9.2 %subtract_reduce_fusion.2 = (f32[64,128]{1,0:T(8,128)S(1)}, f32[64,128]{1,0:T(8,128)S(1)}, f32[64,128,128]{2,1,0:T(8,128)S(1)}) fusion(f32[64,128,128]{2,1,0:T(8,128)S(1)} %multiply_reduce_fusion.11, f32[64,128]{1,0:T(8,128)S(1)} %bitcast.118, f32[64,128]{1,0:T(8,128)S(1)} %bitcast.115, f32[64,128,128]{2,1,0:T(8,128)S(1)} %fusion.72, ...), kind=kLoop, calls=%fused_computation.59.clone.1 | loop fusion | flops 38780928 | bytes 12845056 | tf_op jit(solution)/shard_map/while/body/eval_jaxpr/vmap()/reduce_sum | solution.py:38
  190.3 8.5 %multiply_reduce_fusion.12 = (f32[64,3,128]{2,1,0:T(4,128)S(1)}, f32[64,3,128]{2,1,0:T(4,128)S(1)}) fusion(f32[64,128,128]{2,1,0:T(8,128)S(1)} %get-tuple-element.365, f32[64,128,128]{2,1,0:T(8,128)S(1)} %add_sqrt_fusion.5, f32[64,3,128]{2,1,0:T(4,128)S(1)} %get-tuple-element.356, f32[64,3,128]{2,1,0:T(4,128)S(1)} %get-tuple-element.357), kind=kLoop, calls=%fused_computation.44.clone.1 | loop fusion | flops 15679488 | bytes 8781824 | tf_op jit(solution)/shard_map/while/body/eval_jaxpr/vmap()/reduce_sum | solution.py:38
  210.8 8.0 multiply_reduce_fusion.11
  219.0 9.2 %subtract_reduce_fusion.2 = (f32[64,128]{1,0:T(8,128)S(1)}, f32[64,128]{1,0:T(8,128)S(1)}, f32[64,128,128]{2,1,0:T(8,128)S(1)}) fusion(f32[64,128,128]{2,1,0:T(8,128)S(1)} %multiply_reduce_fusion.11, f32[64,128]{1,0:T(8,128)S(1)} %bitcast.118, f32[64,128]{1,0:T(8,128)S(1)} %bitcast.115, f32[64,128,128]{2,1,0:T(8,128)S(1)} %fusion.72, ...), kind=kLoop, calls=%fused_computation.59.clone.1 | loop fusion | flops 38780928 | bytes 12845056 | tf_op jit(solution)/shard_map/while/body/eval_jaxpr/vmap()/reduce_sum | solution.py:38
  228.2 8.5 %multiply_reduce_fusion.12 = (f32[64,3,128]{2,1,0:T(4,128)S(1)}, f32[64,3,128]{2,1,0:T(4,128)S(1)}) fusion(f32[64,128,128]{2,1,0:T(8,128)S(1)} %get-tuple-element.365, f32[64,128,128]{2,1,0:T(8,128)S(1)} %add_sqrt_fusion.5, f32[64,3,128]{2,1,0:T(4,128)S(1)} %get-tuple-element.356, f32[64,3,128]{2,1,0:T(4,128)S(1)} %get-tuple-element.357), kind=kLoop, calls=%fused_computation.44.clone.1 | loop fusion | flops 15679488 | bytes 8781824 | tf_op jit(solution)/shard_map/while/body/eval_jaxpr/vmap()/reduce_sum | solution.py:38
  248.7 8.0 multiply_reduce_fusion.11
  256.9 9.2 %subtract_reduce_fusion.2 = (f32[64,128]{1,0:T(8,128)S(1)}, f32[64,128]{1,0:T(8,128)S(1)}, f32[64,128,128]{2,1,0:T(8,128)S(1)}) fusion(f32[64,128,128]{2,1,0:T(8,128)S(1)} %multiply_reduce_fusion.11, f32[64,128]{1,0:T(8,128)S(1)} %bitcast.118, f32[64,128]{1,0:T(8,128)S(1)} %bitcast.115, f32[64,128,128]{2,1,0:T(8,128)S(1)} %fusion.72, ...), kind=kLoop, calls=%fused_computation.59.clone.1 | loop fusion | flops 38780928 | bytes 12845056 | tf_op jit(solution)/shard_map/while/body/eval_jaxpr/vmap()/reduce_sum | solution.py:38
  266.1 8.5 %multiply_reduce_fusion.12 = (f32[64,3,128]{2,1,0:T(4,128)S(1)}, f32[64,3,128]{2,1,0:T(4,128)S(1)}) fusion(f32[64,128,128]{2,1,0:T(8,128)S(1)} %get-tuple-element.365, f32[64,128,128]{2,1,0:T(8,128)S(1)} %add_sqrt_fusion.5, f32[64,3,128]{2,1,0:T(4,128)S(1)} %get-tuple-element.356, f32[64,3,128]{2,1,0:T(4,128)S(1)} %get-tuple-element.357), kind=kLoop, calls=%fused_computation.44.clone.1 | loop fusion | flops 15679488 | bytes 8781824 | tf_op jit(solution)/shard_map/while/body/eval_jaxpr/vmap()/reduce_sum | solution.py:38
  286.6 8.0 multiply_reduce_fusion.11
  294.8 9.2 %subtract_reduce_fusion.2 = (f32[64,128]{1,0:T(8,128)S(1)}, f32[64,128]{1,0:T(8,128)S(1)}, f32[64,128,128]{2,1,0:T(8,128)S(1)}) fusion(f32[64,128,128]{2,1,0:T(8,128)S(1)} %multiply_reduce_fusion.11, f32[64,128]{1,0:T(8,128)S(1)} %bitcast.118, f32[64,128]{1,0:T(8,128)S(1)} %bitcast.115, f32[64,128,128]{2,1,0:T(8,128)S(1)} %fusion.72, ...), kind=kLoop, calls=%fused_computation.59.clone.1 | loop fusion | flops 38780928 | bytes 12845056 | tf_op jit(solution)/shard_map/while/body/eval_jaxpr/vmap()/reduce_sum | solution.py:38
  304.0 8.5 %multiply_reduce_fusion.12 = (f32[64,3,128]{2,1,0:T(4,128)S(1)}, f32[64,3,128]{2,1,0:T(4,128)S(1)}) fusion(f32[64,128,128]{2,1,0:T(8,128)S(1)} %get-tuple-element.365, f32[64,128,128]{2,1,0:T(8,128)S(1)} %add_sqrt_fusion.5, f32[64,3,128]{2,1,0:T(4,128)S(1)} %get-tuple-element.356, f32[64,3,128]{2,1,0:T(4,128)S(1)} %get-tuple-element.357), kind=kLoop, calls=%fused_computation.44.clone.1 | loop fusion | flops 15679488 | bytes 8781824 | tf_op jit(solution)/shard_map/while/body/eval_jaxpr/vmap()/reduce_sum | solution.py:38
  319.2 4.1 fusion.72
  324.5 8.0 multiply_reduce_fusion.11
  332.6 9.2 %subtract_reduce_fusion.2 = (f32[64,128]{1,0:T(8,128)S(1)}, f32[64,128]{1,0:T(8,128)S(1)}, f32[64,128,128]{2,1,0:T(8,128)S(1)}) fusion(f32[64,128,128]{2,1,0:T(8,128)S(1)} %multiply_reduce_fusion.11, f32[64,128]{1,0:T(8,128)S(1)} %bitcast.118, f32[64,128]{1,0:T(8,128)S(1)} %bitcast.115, f32[64,128,128]{2,1,0:T(8,128)S(1)} %fusion.72, ...), kind=kLoop, calls=%fused_computation.59.clone.1 | loop fusion | flops 38780928 | bytes 12845056 | tf_op jit(solution)/shard_map/while/body/eval_jaxpr/vmap()/reduce_sum | solution.py:38
  341.8 8.5 %multiply_reduce_fusion.12 = (f32[64,3,128]{2,1,0:T(4,128)S(1)}, f32[64,3,128]{2,1,0:T(4,128)S(1)}) fusion(f32[64,128,128]{2,1,0:T(8,128)S(1)} %get-tuple-element.365, f32[64,128,128]{2,1,0:T(8,128)S(1)} %add_sqrt_fusion.5, f32[64,3,128]{2,1,0:T(4,128)S(1)} %get-tuple-element.356, f32[64,3,128]{2,1,0:T(4,128)S(1)} %get-tuple-element.357), kind=kLoop, calls=%fused_computation.44.clone.1 | loop fusion | flops 15679488 | bytes 8781824 | tf_op jit(solution)/shard_map/while/body/eval_jaxpr/vmap()/reduce_sum | solution.py:38
  357.1 4.1 fusion.72
  362.3 8.0 multiply_reduce_fusion.11
  370.5 9.2 %subtract_reduce_fusion.2 = (f32[64,128]{1,0:T(8,128)S(1)}, f32[64,128]{1,0:T(8,128)S(1)}, f32[64,128,128]{2,1,0:T(8,128)S(1)}) fusion(f32[64,128,128]{2,1,0:T(8,128)S(1)} %multiply_reduce_fusion.11, f32[64,128]{1,0:T(8,128)S(1)} %bitcast.118, f32[64,128]{1,0:T(8,128)S(1)} %bitcast.115, f32[64,128,128]{2,1,0:T(8,128)S(1)} %fusion.72, ...), kind=kLoop, calls=%fused_computation.59.clone.1 | loop fusion | flops 38780928 | bytes 12845056 | tf_op jit(solution)/shard_map/while/body/eval_jaxpr/vmap()/reduce_sum | solution.py:38
  379.7 8.5 %multiply_reduce_fusion.12 = (f32[64,3,128]{2,1,0:T(4,128)S(1)}, f32[64,3,128]{2,1,0:T(4,128)S(1)}) fusion(f32[64,128,128]{2,1,0:T(8,128)S(1)} %get-tuple-element.365, f32[64,128,128]{2,1,0:T(8,128)S(1)} %add_sqrt_fusion.5, f32[64,3,128]{2,1,0:T(4,128)S(1)} %get-tuple-element.356, f32[64,3,128]{2,1,0:T(4,128)S(1)} %get-tuple-element.357), kind=kLoop, calls=%fused_computation.44.clone.1 | loop fusion | flops 15679488 | bytes 8781824 | tf_op jit(solution)/shard_map/while/body/eval_jaxpr/vmap()/reduce_sum | solution.py:38
  400.2 8.0 multiply_reduce_fusion.11
  408.4 9.2 %subtract_reduce_fusion.2 = (f32[64,128]{1,0:T(8,128)S(1)}, f32[64,128]{1,0:T(8,128)S(1)}, f32[64,128,128]{2,1,0:T(8,128)S(1)}) fusion(f32[64,128,128]{2,1,0:T(8,128)S(1)} %multiply_reduce_fusion.11, f32[64,128]{1,0:T(8,128)S(1)} %bitcast.118, f32[64,128]{1,0:T(8,128)S(1)} %bitcast.115, f32[64,128,128]{2,1,0:T(8,128)S(1)} %fusion.72, ...), kind=kLoop, calls=%fused_computation.59.clone.1 | loop fusion | flops 38780928 | bytes 12845056 | tf_op jit(solution)/shard_map/while/body/eval_jaxpr/vmap()/reduce_sum | solution.py:38
  417.6 8.5 %multiply_reduce_fusion.12 = (f32[64,3,128]{2,1,0:T(4,128)S(1)}, f32[64,3,128]{2,1,0:T(4,128)S(1)}) fusion(f32[64,128,128]{2,1,0:T(8,128)S(1)} %get-tuple-element.365, f32[64,128,128]{2,1,0:T(8,128)S(1)} %add_sqrt_fusion.5, f32[64,3,128]{2,1,0:T(4,128)S(1)} %get-tuple-element.356, f32[64,3,128]{2,1,0:T(4,128)S(1)} %get-tuple-element.357), kind=kLoop, calls=%fused_computation.44.clone.1 | loop fusion | flops 15679488 | bytes 8781824 | tf_op jit(solution)/shard_map/while/body/eval_jaxpr/vmap()/reduce_sum | solution.py:38
  438.1 8.0 multiply_reduce_fusion.11
  446.3 9.2 %subtract_reduce_fusion.2 = (f32[64,128]{1,0:T(8,128)S(1)}, f32[64,128]{1,0:T(8,128)S(1)}, f32[64,128,128]{2,1,0:T(8,128)S(1)}) fusion(f32[64,128,128]{2,1,0:T(8,128)S(1)} %multiply_reduce_fusion.11, f32[64,128]{1,0:T(8,128)S(1)} %bitcast.118, f32[64,128]{1,0:T(8,128)S(1)} %bitcast.115, f32[64,128,128]{2,1,0:T(8,128)S(1)} %fusion.72, ...), kind=kLoop, calls=%fused_computation.59.clone.1 | loop fusion | flops 38780928 | bytes 12845056 | tf_op jit(solution)/shard_map/while/body/eval_jaxpr/vmap()/reduce_sum | solution.py:38
  455.5 8.5 %multiply_reduce_fusion.12 = (f32[64,3,128]{2,1,0:T(4,128)S(1)}, f32[64,3,128]{2,1,0:T(4,128)S(1)}) fusion(f32[64,128,128]{2,1,0:T(8,128)S(1)} %get-tuple-element.365, f32[64,128,128]{2,1,0:T(8,128)S(1)} %add_sqrt_fusion.5, f32[64,3,128]{2,1,0:T(4,128)S(1)} %get-tuple-element.356, f32[64,3,128]{2,1,0:T(4,128)S(1)} %get-tuple-element.357), kind=kLoop, calls=%fused_computation.44.clone.1 | loop fusion | flops 15679488 | bytes 8781824 | tf_op jit(solution)/shard_map/while/body/eval_jaxpr/vmap()/reduce_sum | solution.py:38
  470.7 4.1 fusion.72
  476.0 8.0 multiply_reduce_fusion.11
  484.2 9.2 %subtract_reduce_fusion.2 = (f32[64,128]{1,0:T(8,128)S(1)}, f32[64,128]{1,0:T(8,128)S(1)}, f32[64,128,128]{2,1,0:T(8,128)S(1)}) fusion(f32[64,128,128]{2,1,0:T(8,128)S(1)} %multiply_reduce_fusion.11, f32[64,128]{1,0:T(8,128)S(1)} %bitcast.118, f32[64,128]{1,0:T(8,128)S(1)} %bitcast.115, f32[64,128,128]{2,1,0:T(8,128)S(1)} %fusion.72, ...), kind=kLoop, calls=%fused_computation.59.clone.1 | loop fusion | flops 38780928 | bytes 12845056 | tf_op jit(solution)/shard_map/while/body/eval_jaxpr/vmap()/reduce_sum | solution.py:38
  493.4 8.5 %multiply_reduce_fusion.12 = (f32[64,3,128]{2,1,0:T(4,128)S(1)}, f32[64,3,128]{2,1,0:T(4,128)S(1)}) fusion(f32[64,128,128]{2,1,0:T(8,128)S(1)} %get-tuple-element.365, f32[64,128,128]{2,1,0:T(8,128)S(1)} %add_sqrt_fusion.5, f32[64,3,128]{2,1,0:T(4,128)S(1)} %get-tuple-element.356, f32[64,3,128]{2,1,0:T(4,128)S(1)} %get-tuple-element.357), kind=kLoop, calls=%fused_computation.44.clone.1 | loop fusion | flops 15679488 | bytes 8781824 | tf_op jit(solution)/shard_map/while/body/eval_jaxpr/vmap()/reduce_sum | solution.py:38
  508.6 4.1 fusion.72
  513.9 8.0 multiply_reduce_fusion.11
  522.0 9.2 %subtract_reduce_fusion.2 = (f32[64,128]{1,0:T(8,128)S(1)}, f32[64,128]{1,0:T(8,128)S(1)}, f32[64,128,128]{2,1,0:T(8,128)S(1)}) fusion(f32[64,128,128]{2,1,0:T(8,128)S(1)} %multiply_reduce_fusion.11, f32[64,128]{1,0:T(8,128)S(1)} %bitcast.118, f32[64,128]{1,0:T(8,128)S(1)} %bitcast.115, f32[64,128,128]{2,1,0:T(8,128)S(1)} %fusion.72, ...), kind=kLoop, calls=%fused_computation.59.clone.1 | loop fusion | flops 38780928 | bytes 12845056 | tf_op jit(solution)/shard_map/while/body/eval_jaxpr/vmap()/reduce_sum | solution.py:38
  531.2 8.5 %multiply_reduce_fusion.12 = (f32[64,3,128]{2,1,0:T(4,128)S(1)}, f32[64,3,128]{2,1,0:T(4,128)S(1)}) fusion(f32[64,128,128]{2,1,0:T(8,128)S(1)} %get-tuple-element.365, f32[64,128,128]{2,1,0:T(8,128)S(1)} %add_sqrt_fusion.5, f32[64,3,128]{2,1,0:T(4,128)S(1)} %get-tuple-element.356, f32[64,3,128]{2,1,0:T(4,128)S(1)} %get-tuple-element.357), kind=kLoop, calls=%fused_computation.44.clone.1 | loop fusion | flops 15679488 | bytes 8781824 | tf_op jit(solution)/shard_map/while/body/eval_jaxpr/vmap()/reduce_sum | solution.py:38
  546.5 4.1 fusion.72
  551.7 8.0 multiply_reduce_fusion.11
  559.9 9.2 %subtract_reduce_fusion.2 = (f32[64,128]{1,0:T(8,128)S(1)}, f32[64,128]{1,0:T(8,128)S(1)}, f32[64,128,128]{2,1,0:T(8,128)S(1)}) fusion(f32[64,128,128]{2,1,0:T(8,128)S(1)} %multiply_reduce_fusion.11, f32[64,128]{1,0:T(8,128)S(1)} %bitcast.118, f32[64,128]{1,0:T(8,128)S(1)} %bitcast.115, f32[64,128,128]{2,1,0:T(8,128)S(1)} %fusion.72, ...), kind=kLoop, calls=%fused_computation.59.clone.1 | loop fusion | flops 38780928 | bytes 12845056 | tf_op jit(solution)/shard_map/while/body/eval_jaxpr/vmap()/reduce_sum | solution.py:38
  569.1 8.5 %multiply_reduce_fusion.12 = (f32[64,3,128]{2,1,0:T(4,128)S(1)}, f32[64,3,128]{2,1,0:T(4,128)S(1)}) fusion(f32[64,128,128]{2,1,0:T(8,128)S(1)} %get-tuple-element.365, f32[64,128,128]{2,1,0:T(8,128)S(1)} %add_sqrt_fusion.5, f32[64,3,128]{2,1,0:T(4,128)S(1)} %get-tuple-element.356, f32[64,3,128]{2,1,0:T(4,128)S(1)} %get-tuple-element.357), kind=kLoop, calls=%fused_computation.44.clone.1 | loop fusion | flops 15679488 | bytes 8781824 | tf_op jit(solution)/shard_map/while/body/eval_jaxpr/vmap()/reduce_sum | solution.py:38
  589.6 8.0 multiply_reduce_fusion.11
  597.8 9.2 %subtract_reduce_fusion.2 = (f32[64,128]{1,0:T(8,128)S(1)}, f32[64,128]{1,0:T(8,128)S(1)}, f32[64,128,128]{2,1,0:T(8,128)S(1)}) fusion(f32[64,128,128]{2,1,0:T(8,128)S(1)} %multiply_reduce_fusion.11, f32[64,128]{1,0:T(8,128)S(1)} %bitcast.118, f32[64,128]{1,0:T(8,128)S(1)} %bitcast.115, f32[64,128,128]{2,1,0:T(8,128)S(1)} %fusion.72, ...), kind=kLoop, calls=%fused_computation.59.clone.1 | loop fusion | flops 38780928 | bytes 12845056 | tf_op jit(solution)/shard_map/while/body/eval_jaxpr/vmap()/reduce_sum | solution.py:38
  607.0 8.5 %multiply_reduce_fusion.12 = (f32[64,3,128]{2,1,0:T(4,128)S(1)}, f32[64,3,128]{2,1,0:T(4,128)S(1)}) fusion(f32[64,128,128]{2,1,0:T(8,128)S(1)} %get-tuple-element.365, f32[64,128,128]{2,1,0:T(8,128)S(1)} %add_sqrt_fusion.5, f32[64,3,128]{2,1,0:T(4,128)S(1)} %get-tuple-element.356, f32[64,3,128]{2,1,0:T(4,128)S(1)} %get-tuple-element.357), kind=kLoop, calls=%fused_computation.44.clone.1 | loop fusion | flops 15679488 | bytes 8781824 | tf_op jit(solution)/shard_map/while/body/eval_jaxpr/vmap()/reduce_sum | solution.py:38
  627.5 8.0 multiply_reduce_fusion.11
  635.7 9.2 %subtract_reduce_fusion.2 = (f32[64,128]{1,0:T(8,128)S(1)}, f32[64,128]{1,0:T(8,128)S(1)}, f32[64,128,128]{2,1,0:T(8,128)S(1)}) fusion(f32[64,128,128]{2,1,0:T(8,128)S(1)} %multiply_reduce_fusion.11, f32[64,128]{1,0:T(8,128)S(1)} %bitcast.118, f32[64,128]{1,0:T(8,128)S(1)} %bitcast.115, f32[64,128,128]{2,1,0:T(8,128)S(1)} %fusion.72, ...), kind=kLoop, calls=%fused_computation.59.clone.1 | loop fusion | flops 38780928 | bytes 12845056 | tf_op jit(solution)/shard_map/while/body/eval_jaxpr/vmap()/reduce_sum | solution.py:38
  644.9 8.5 %multiply_reduce_fusion.12 = (f32[64,3,128]{2,1,0:T(4,128)S(1)}, f32[64,3,128]{2,1,0:T(4,128)S(1)}) fusion(f32[64,128,128]{2,1,0:T(8,128)S(1)} %get-tuple-element.365, f32[64,128,128]{2,1,0:T(8,128)S(1)} %add_sqrt_fusion.5, f32[64,3,128]{2,1,0:T(4,128)S(1)} %get-tuple-element.356, f32[64,3,128]{2,1,0:T(4,128)S(1)} %get-tuple-element.357), kind=kLoop, calls=%fused_computation.44.clone.1 | loop fusion | flops 15679488 | bytes 8781824 | tf_op jit(solution)/shard_map/while/body/eval_jaxpr/vmap()/reduce_sum | solution.py:38
  665.4 8.0 multiply_reduce_fusion.11
  673.6 9.2 %subtract_reduce_fusion.2 = (f32[64,128]{1,0:T(8,128)S(1)}, f32[64,128]{1,0:T(8,128)S(1)}, f32[64,128,128]{2,1,0:T(8,128)S(1)}) fusion(f32[64,128,128]{2,1,0:T(8,128)S(1)} %multiply_reduce_fusion.11, f32[64,128]{1,0:T(8,128)S(1)} %bitcast.118, f32[64,128]{1,0:T(8,128)S(1)} %bitcast.115, f32[64,128,128]{2,1,0:T(8,128)S(1)} %fusion.72, ...), kind=kLoop, calls=%fused_computation.59.clone.1 | loop fusion | flops 38780928 | bytes 12845056 | tf_op jit(solution)/shard_map/while/body/eval_jaxpr/vmap()/reduce_sum | solution.py:38
  682.8 8.5 %multiply_reduce_fusion.12 = (f32[64,3,128]{2,1,0:T(4,128)S(1)}, f32[64,3,128]{2,1,0:T(4,128)S(1)}) fusion(f32[64,128,128]{2,1,0:T(8,128)S(1)} %get-tuple-element.365, f32[64,128,128]{2,1,0:T(8,128)S(1)} %add_sqrt_fusion.5, f32[64,3,128]{2,1,0:T(4,128)S(1)} %get-tuple-element.356, f32[64,3,128]{2,1,0:T(4,128)S(1)} %get-tuple-element.357), kind=kLoop, calls=%fused_computation.44.clone.1 | loop fusion | flops 15679488 | bytes 8781824 | tf_op jit(solution)/shard_map/while/body/eval_jaxpr/vmap()/reduce_sum | solution.py:38
  703.3 8.0 multiply_reduce_fusion.11
  711.4 9.2 %subtract_reduce_fusion.2 = (f32[64,128]{1,0:T(8,128)S(1)}, f32[64,128]{1,0:T(8,128)S(1)}, f32[64,128,128]{2,1,0:T(8,128)S(1)}) fusion(f32[64,128,128]{2,1,0:T(8,128)S(1)} %multiply_reduce_fusion.11, f32[64,128]{1,0:T(8,128)S(1)} %bitcast.118, f32[64,128]{1,0:T(8,128)S(1)} %bitcast.115, f32[64,128,128]{2,1,0:T(8,128)S(1)} %fusion.72, ...), kind=kLoop, calls=%fused_computation.59.clone.1 | loop fusion | flops 38780928 | bytes 12845056 | tf_op jit(solution)/shard_map/while/body/eval_jaxpr/vmap()/reduce_sum | solution.py:38
  720.6 8.5 %multiply_reduce_fusion.12 = (f32[64,3,128]{2,1,0:T(4,128)S(1)}, f32[64,3,128]{2,1,0:T(4,128)S(1)}) fusion(f32[64,128,128]{2,1,0:T(8,128)S(1)} %get-tuple-element.365, f32[64,128,128]{2,1,0:T(8,128)S(1)} %add_sqrt_fusion.5, f32[64,3,128]{2,1,0:T(4,128)S(1)} %get-tuple-element.356, f32[64,3,128]{2,1,0:T(4,128)S(1)} %get-tuple-element.357), kind=kLoop, calls=%fused_computation.44.clone.1 | loop fusion | flops 15679488 | bytes 8781824 | tf_op jit(solution)/shard_map/while/body/eval_jaxpr/vmap()/reduce_sum | solution.py:38
  736.3 5.4 collective-permute-done.1
  741.7 4.9 fusion.41
  746.6 69.2 %while.27 = (s32[]{:T(128)}, f32[8,16,4,128]{3,2,1,0:T(4,128)S(1)}, f32[8,16,9,128]{3,1,0,2:T(8,128)}, s32[]{:T(128)}) while((s32[]{:T(128)}, f32[8,16,4,128]{3,2,1,0:T(4,128)S(1)}, f32[8,16,9,128]{3,1,0,2:T(8,128)}, s32[]{:T(128)}) %tuple.104), condition=%wide.region_14.15_spmd, body=%wide.region_9.14_spmd.sunk | while | flops 18925568 | bytes 11239485 | solution.py:147
  815.9 5.3 reduce-scatter.2.cloned.1.call-done
  (642 shorter events, 258.3 us)
Async XLA Ops:
  6.5 82.5 %all-gather.2.cloned.1.call-start = ((), (), s32[]{:S(2)}) async-start(), calls=%async_computation.1 | async-start | bytes 10027008 | tf_op jit(solution)/shard_map/all_gather | solution.py:96
  11.8 809.4 %reduce-scatter.2.cloned.1.call-start = ((), (), s32[]{:S(2)}) async-start(), calls=%async_computation.2 | async-start | bytes 4456448 | tf_op jit(solution)/shard_map/reduce_scatter | solution.py:136
  101.8 11.4 %copy-start.8 = (s32[1,1024,2]{1,2,0:T(2,128)S(1)}, s32[1,1024,2]{1,2,0:T(2,128)}, u32[]{:S(2)}) copy-start(s32[1,1024,2]{1,2,0:T(2,128)} %param.18) | copy-start | bytes 24580
  109.5 13.9 %collective-permute-start = (f32[192,9,128]{2,0,1:T(8,128)}, f32[192,9,128]{2,0,1:T(8,128)S(1)}, u32[]{:S(2)}, u32[]{:S(2)}) collective-permute-start(f32[192,9,128]{2,0,1:T(8,128)} %copy.34), channel_id=1, source_target_pairs={{0,16},{16,32},{32,48},{48,64},{64,80},{80,96},{96,112},{1,17},{17... | collective-permute-start | bytes 2654216 | tf_op jit(solution)/shard_map/ppermute | solution.py:16
  125.9 3.2 copy-start.6
  152.4 8.6 %copy-start.5 = (s32[16,64]{1,0:T(8,128)S(1)}, s32[16,64]{1,0:T(8,128)}, u32[]{:S(2)}) copy-start(s32[16,64]{1,0:T(8,128)} %copy-done.4) | copy-start | bytes 12292 | tf_op jit(solution)/shard_map/while
  152.4 8.6 %copy-start.7 = (s32[16,64]{1,0:T(8,128)S(1)}, s32[16,64]{1,0:T(8,128)}, u32[]{:S(2)}) copy-start(s32[16,64]{1,0:T(8,128)} %copy-done.6) | copy-start | bytes 12292 | tf_op jit(solution)/shard_map/while
  152.4 10.1 %copy-start = (f32[192,512]{1,0:T(8,128)S(1)}, f32[192,512]{1,0:T(8,128)}, u32[]{:S(2)}) copy-start(f32[192,512]{1,0:T(8,128)} %get-tuple-element.382) | copy-start | bytes 1179652 | tf_op jit(solution)/shard_map/while
  163.8 3.2 copy-start.6
  190.3 8.6 %copy-start.5 = (s32[16,64]{1,0:T(8,128)S(1)}, s32[16,64]{1,0:T(8,128)}, u32[]{:S(2)}) copy-start(s32[16,64]{1,0:T(8,128)} %copy-done.4) | copy-start | bytes 12292 | tf_op jit(solution)/shard_map/while
  190.3 8.6 %copy-start.7 = (s32[16,64]{1,0:T(8,128)S(1)}, s32[16,64]{1,0:T(8,128)}, u32[]{:S(2)}) copy-start(s32[16,64]{1,0:T(8,128)} %copy-done.6) | copy-start | bytes 12292 | tf_op jit(solution)/shard_map/while
  190.3 10.1 %copy-start = (f32[192,512]{1,0:T(8,128)S(1)}, f32[192,512]{1,0:T(8,128)}, u32[]{:S(2)}) copy-start(f32[192,512]{1,0:T(8,128)} %get-tuple-element.382) | copy-start | bytes 1179652 | tf_op jit(solution)/shard_map/while
  201.6 3.2 copy-start.6
  228.2 8.6 %copy-start.5 = (s32[16,64]{1,0:T(8,128)S(1)}, s32[16,64]{1,0:T(8,128)}, u32[]{:S(2)}) copy-start(s32[16,64]{1,0:T(8,128)} %copy-done.4) | copy-start | bytes 12292 | tf_op jit(solution)/shard_map/while
  228.2 8.6 %copy-start.7 = (s32[16,64]{1,0:T(8,128)S(1)}, s32[16,64]{1,0:T(8,128)}, u32[]{:S(2)}) copy-start(s32[16,64]{1,0:T(8,128)} %copy-done.6) | copy-start | bytes 12292 | tf_op jit(solution)/shard_map/while
  228.2 10.1 %copy-start = (f32[192,512]{1,0:T(8,128)S(1)}, f32[192,512]{1,0:T(8,128)}, u32[]{:S(2)}) copy-start(f32[192,512]{1,0:T(8,128)} %get-tuple-element.382) | copy-start | bytes 1179652 | tf_op jit(solution)/shard_map/while
  239.5 3.2 copy-start.6
  266.1 8.6 %copy-start.5 = (s32[16,64]{1,0:T(8,128)S(1)}, s32[16,64]{1,0:T(8,128)}, u32[]{:S(2)}) copy-start(s32[16,64]{1,0:T(8,128)} %copy-done.4) | copy-start | bytes 12292 | tf_op jit(solution)/shard_map/while
  266.1 8.6 %copy-start.7 = (s32[16,64]{1,0:T(8,128)S(1)}, s32[16,64]{1,0:T(8,128)}, u32[]{:S(2)}) copy-start(s32[16,64]{1,0:T(8,128)} %copy-done.6) | copy-start | bytes 12292 | tf_op jit(solution)/shard_map/while
  266.1 10.1 %copy-start = (f32[192,512]{1,0:T(8,128)S(1)}, f32[192,512]{1,0:T(8,128)}, u32[]{:S(2)}) copy-start(f32[192,512]{1,0:T(8,128)} %get-tuple-element.382) | copy-start | bytes 1179652 | tf_op jit(solution)/shard_map/while
  277.4 3.2 copy-start.6
  303.9 8.6 %copy-start.5 = (s32[16,64]{1,0:T(8,128)S(1)}, s32[16,64]{1,0:T(8,128)}, u32[]{:S(2)}) copy-start(s32[16,64]{1,0:T(8,128)} %copy-done.4) | copy-start | bytes 12292 | tf_op jit(solution)/shard_map/while
  303.9 8.6 %copy-start.7 = (s32[16,64]{1,0:T(8,128)S(1)}, s32[16,64]{1,0:T(8,128)}, u32[]{:S(2)}) copy-start(s32[16,64]{1,0:T(8,128)} %copy-done.6) | copy-start | bytes 12292 | tf_op jit(solution)/shard_map/while
  304.0 10.1 %copy-start = (f32[192,512]{1,0:T(8,128)S(1)}, f32[192,512]{1,0:T(8,128)}, u32[]{:S(2)}) copy-start(f32[192,512]{1,0:T(8,128)} %get-tuple-element.382) | copy-start | bytes 1179652 | tf_op jit(solution)/shard_map/while
  315.3 3.2 copy-start.6
  341.8 8.6 %copy-start.5 = (s32[16,64]{1,0:T(8,128)S(1)}, s32[16,64]{1,0:T(8,128)}, u32[]{:S(2)}) copy-start(s32[16,64]{1,0:T(8,128)} %copy-done.4) | copy-start | bytes 12292 | tf_op jit(solution)/shard_map/while
  341.8 8.6 %copy-start.7 = (s32[16,64]{1,0:T(8,128)S(1)}, s32[16,64]{1,0:T(8,128)}, u32[]{:S(2)}) copy-start(s32[16,64]{1,0:T(8,128)} %copy-done.6) | copy-start | bytes 12292 | tf_op jit(solution)/shard_map/while
  341.8 10.1 %copy-start = (f32[192,512]{1,0:T(8,128)S(1)}, f32[192,512]{1,0:T(8,128)}, u32[]{:S(2)}) copy-start(f32[192,512]{1,0:T(8,128)} %get-tuple-element.382) | copy-start | bytes 1179652 | tf_op jit(solution)/shard_map/while
  353.2 3.2 copy-start.6
  379.7 8.6 %copy-start.5 = (s32[16,64]{1,0:T(8,128)S(1)}, s32[16,64]{1,0:T(8,128)}, u32[]{:S(2)}) copy-start(s32[16,64]{1,0:T(8,128)} %copy-done.4) | copy-start | bytes 12292 | tf_op jit(solution)/shard_map/while
  379.7 8.6 %copy-start.7 = (s32[16,64]{1,0:T(8,128)S(1)}, s32[16,64]{1,0:T(8,128)}, u32[]{:S(2)}) copy-start(s32[16,64]{1,0:T(8,128)} %copy-done.6) | copy-start | bytes 12292 | tf_op jit(solution)/shard_map/while
  379.7 10.1 %copy-start = (f32[192,512]{1,0:T(8,128)S(1)}, f32[192,512]{1,0:T(8,128)}, u32[]{:S(2)}) copy-start(f32[192,512]{1,0:T(8,128)} %get-tuple-element.382) | copy-start | bytes 1179652 | tf_op jit(solution)/shard_map/while
  391.0 3.2 copy-start.6
  417.6 8.6 %copy-start.5 = (s32[16,64]{1,0:T(8,128)S(1)}, s32[16,64]{1,0:T(8,128)}, u32[]{:S(2)}) copy-start(s32[16,64]{1,0:T(8,128)} %copy-done.4) | copy-start | bytes 12292 | tf_op jit(solution)/shard_map/while
  417.6 8.6 %copy-start.7 = (s32[16,64]{1,0:T(8,128)S(1)}, s32[16,64]{1,0:T(8,128)}, u32[]{:S(2)}) copy-start(s32[16,64]{1,0:T(8,128)} %copy-done.6) | copy-start | bytes 12292 | tf_op jit(solution)/shard_map/while
  417.6 10.1 %copy-start = (f32[192,512]{1,0:T(8,128)S(1)}, f32[192,512]{1,0:T(8,128)}, u32[]{:S(2)}) copy-start(f32[192,512]{1,0:T(8,128)} %get-tuple-element.382) | copy-start | bytes 1179652 | tf_op jit(solution)/shard_map/while
  428.9 3.2 copy-start.6
  455.5 8.6 %copy-start.5 = (s32[16,64]{1,0:T(8,128)S(1)}, s32[16,64]{1,0:T(8,128)}, u32[]{:S(2)}) copy-start(s32[16,64]{1,0:T(8,128)} %copy-done.4) | copy-start | bytes 12292 | tf_op jit(solution)/shard_map/while
  455.5 8.6 %copy-start.7 = (s32[16,64]{1,0:T(8,128)S(1)}, s32[16,64]{1,0:T(8,128)}, u32[]{:S(2)}) copy-start(s32[16,64]{1,0:T(8,128)} %copy-done.6) | copy-start | bytes 12292 | tf_op jit(solution)/shard_map/while
  455.5 10.1 %copy-start = (f32[192,512]{1,0:T(8,128)S(1)}, f32[192,512]{1,0:T(8,128)}, u32[]{:S(2)}) copy-start(f32[192,512]{1,0:T(8,128)} %get-tuple-element.382) | copy-start | bytes 1179652 | tf_op jit(solution)/shard_map/while
  466.8 3.2 copy-start.6
  493.3 8.6 %copy-start.5 = (s32[16,64]{1,0:T(8,128)S(1)}, s32[16,64]{1,0:T(8,128)}, u32[]{:S(2)}) copy-start(s32[16,64]{1,0:T(8,128)} %copy-done.4) | copy-start | bytes 12292 | tf_op jit(solution)/shard_map/while
  493.3 8.6 %copy-start.7 = (s32[16,64]{1,0:T(8,128)S(1)}, s32[16,64]{1,0:T(8,128)}, u32[]{:S(2)}) copy-start(s32[16,64]{1,0:T(8,128)} %copy-done.6) | copy-start | bytes 12292 | tf_op jit(solution)/shard_map/while
  493.4 10.1 %copy-start = (f32[192,512]{1,0:T(8,128)S(1)}, f32[192,512]{1,0:T(8,128)}, u32[]{:S(2)}) copy-start(f32[192,512]{1,0:T(8,128)} %get-tuple-element.382) | copy-start | bytes 1179652 | tf_op jit(solution)/shard_map/while
  504.7 3.2 copy-start.6
  531.2 8.6 %copy-start.5 = (s32[16,64]{1,0:T(8,128)S(1)}, s32[16,64]{1,0:T(8,128)}, u32[]{:S(2)}) copy-start(s32[16,64]{1,0:T(8,128)} %copy-done.4) | copy-start | bytes 12292 | tf_op jit(solution)/shard_map/while
  531.2 8.6 %copy-start.7 = (s32[16,64]{1,0:T(8,128)S(1)}, s32[16,64]{1,0:T(8,128)}, u32[]{:S(2)}) copy-start(s32[16,64]{1,0:T(8,128)} %copy-done.6) | copy-start | bytes 12292 | tf_op jit(solution)/shard_map/while
  531.2 10.1 %copy-start = (f32[192,512]{1,0:T(8,128)S(1)}, f32[192,512]{1,0:T(8,128)}, u32[]{:S(2)}) copy-start(f32[192,512]{1,0:T(8,128)} %get-tuple-element.382) | copy-start | bytes 1179652 | tf_op jit(solution)/shard_map/while
  569.1 8.6 %copy-start.5 = (s32[16,64]{1,0:T(8,128)S(1)}, s32[16,64]{1,0:T(8,128)}, u32[]{:S(2)}) copy-start(s32[16,64]{1,0:T(8,128)} %copy-done.4) | copy-start | bytes 12292 | tf_op jit(solution)/shard_map/while
  569.1 8.6 %copy-start.7 = (s32[16,64]{1,0:T(8,128)S(1)}, s32[16,64]{1,0:T(8,128)}, u32[]{:S(2)}) copy-start(s32[16,64]{1,0:T(8,128)} %copy-done.6) | copy-start | bytes 12292 | tf_op jit(solution)/shard_map/while
  569.1 10.1 %copy-start = (f32[192,512]{1,0:T(8,128)S(1)}, f32[192,512]{1,0:T(8,128)}, u32[]{:S(2)}) copy-start(f32[192,512]{1,0:T(8,128)} %get-tuple-element.382) | copy-start | bytes 1179652 | tf_op jit(solution)/shard_map/while
  607.0 8.6 %copy-start.5 = (s32[16,64]{1,0:T(8,128)S(1)}, s32[16,64]{1,0:T(8,128)}, u32[]{:S(2)}) copy-start(s32[16,64]{1,0:T(8,128)} %copy-done.4) | copy-start | bytes 12292 | tf_op jit(solution)/shard_map/while
  607.0 8.6 %copy-start.7 = (s32[16,64]{1,0:T(8,128)S(1)}, s32[16,64]{1,0:T(8,128)}, u32[]{:S(2)}) copy-start(s32[16,64]{1,0:T(8,128)} %copy-done.6) | copy-start | bytes 12292 | tf_op jit(solution)/shard_map/while
  607.0 10.1 %copy-start = (f32[192,512]{1,0:T(8,128)S(1)}, f32[192,512]{1,0:T(8,128)}, u32[]{:S(2)}) copy-start(f32[192,512]{1,0:T(8,128)} %get-tuple-element.382) | copy-start | bytes 1179652 | tf_op jit(solution)/shard_map/while
  644.9 8.6 %copy-start.5 = (s32[16,64]{1,0:T(8,128)S(1)}, s32[16,64]{1,0:T(8,128)}, u32[]{:S(2)}) copy-start(s32[16,64]{1,0:T(8,128)} %copy-done.4) | copy-start | bytes 12292 | tf_op jit(solution)/shard_map/while
  644.9 8.6 %copy-start.7 = (s32[16,64]{1,0:T(8,128)S(1)}, s32[16,64]{1,0:T(8,128)}, u32[]{:S(2)}) copy-start(s32[16,64]{1,0:T(8,128)} %copy-done.6) | copy-start | bytes 12292 | tf_op jit(solution)/shard_map/while
  644.9 10.1 %copy-start = (f32[192,512]{1,0:T(8,128)S(1)}, f32[192,512]{1,0:T(8,128)}, u32[]{:S(2)}) copy-start(f32[192,512]{1,0:T(8,128)} %get-tuple-element.382) | copy-start | bytes 1179652 | tf_op jit(solution)/shard_map/while
  682.7 8.6 %copy-start.5 = (s32[16,64]{1,0:T(8,128)S(1)}, s32[16,64]{1,0:T(8,128)}, u32[]{:S(2)}) copy-start(s32[16,64]{1,0:T(8,128)} %copy-done.4) | copy-start | bytes 12292 | tf_op jit(solution)/shard_map/while
  682.7 8.6 %copy-start.7 = (s32[16,64]{1,0:T(8,128)S(1)}, s32[16,64]{1,0:T(8,128)}, u32[]{:S(2)}) copy-start(s32[16,64]{1,0:T(8,128)} %copy-done.6) | copy-start | bytes 12292 | tf_op jit(solution)/shard_map/while
  682.7 10.1 %copy-start = (f32[192,512]{1,0:T(8,128)S(1)}, f32[192,512]{1,0:T(8,128)}, u32[]{:S(2)}) copy-start(f32[192,512]{1,0:T(8,128)} %get-tuple-element.382) | copy-start | bytes 1179652 | tf_op jit(solution)/shard_map/while
  720.6 8.6 %copy-start.5 = (s32[16,64]{1,0:T(8,128)S(1)}, s32[16,64]{1,0:T(8,128)}, u32[]{:S(2)}) copy-start(s32[16,64]{1,0:T(8,128)} %copy-done.4) | copy-start | bytes 12292 | tf_op jit(solution)/shard_map/while
  720.6 8.6 %copy-start.7 = (s32[16,64]{1,0:T(8,128)S(1)}, s32[16,64]{1,0:T(8,128)}, u32[]{:S(2)}) copy-start(s32[16,64]{1,0:T(8,128)} %copy-done.6) | copy-start | bytes 12292 | tf_op jit(solution)/shard_map/while
  720.6 10.1 %copy-start = (f32[192,512]{1,0:T(8,128)S(1)}, f32[192,512]{1,0:T(8,128)}, u32[]{:S(2)}) copy-start(f32[192,512]{1,0:T(8,128)} %get-tuple-element.382) | copy-start | bytes 1179652 | tf_op jit(solution)/shard_map/while
  732.0 9.7 %collective-permute-start.1 = (f32[192,512]{1,0:T(8,128)S(1)}, f32[192,512]{1,0:T(8,128)S(1)}, u32[]{:S(2)}, u32[]{:S(2)}) collective-permute-start(f32[192,512]{1,0:T(8,128)S(1)} %slice.109), channel_id=1, source_target_pairs={{16,0},{32,16},{48,32},{64,48},{80,64},{96,80},{112,96},{17,1},{33... | collective-permute-start | bytes 1179656 | tf_op jit(solution)/shard_map/ppermute | solution.py:16
  (54 other events, 98.3 us)
Sparse Core Ops, SparseCore 0:
  12.0 77.0 all-gather.1
  746.8 74.3 reduce-scatter.1
where the time goes:
time: 836 us; the launch traced here: 830 us
  other arithmetic  564 us (67%)
  local copies, waits for them, and re-layouts  123 us (15%)
  waiting for transfers between devices  74.5 us (9%)
  matrix products  23.4 us (3%)
  blocking collectives  19.5 us (2%)
  between operations  14.2 us (2%)
    reduce_sum x16, other arithmetic, tile_pair(): jnp.sum(viscous - conduct, 0)[None]  147 us
    reduce_sum x16, other arithmetic, tile_pair(): jnp.sum(force, 1)  135 us
    reduce_sum x16, other arithmetic, tile_pair(): along = jnp.sum(unit * relative, 0)  128 us
    reduce_sum x16, other arithmetic, tile_pair(): radius = jnp.sqrt(jnp.sum(offset * offset, 0) + 0.01)  66.2 us
    all_gather x1, waiting for transfers between devices, per_device(): group_data = lax.all_gather(owned, 'tile', axis=0, tiled=True)  54.9 us
    gather x16, local copies, waits for them, and re-layouts, consume(): reachable[second_index]  39.7 us
    all_gather x1, blocking collectives, per_device(): tables = lax.all_gather(exported_tile_places, 'tile', axis=0, tiled=True)  19.5 us
    mul x8, other arithmetic, tile_self(): (repulse * weight - friction * weight * weight * along + noise_amp * weig...  19.2 us
  transfers between devices with their start and end apart: 4, of which 4 were waited for; matrix products, arithmetic and copies ran while one was open for 9% of the time, Pallas kernels for 0%

commit v1 on v0

v1 whole, which is shorter than its diff:
```python
import functools

import jax
import jax.numpy as jnp
from jax import lax
from jax.experimental import pallas as pl
from jax.experimental.pallas import tpu as pltpu
from jax.sharding import PartitionSpec as P

friction = 0.45
noise_amp = 0.3
conductivity = 0.1
MODULUS = 65521
MIDDLE = 0.8

F32 = jnp.float32
BF16 = jnp.bfloat16
I32 = jnp.int32
MESH = pl.DeviceIdType.MESH
MIB = 2**20

HASH_UNIT = 2.0**32
FORCE_UNIT = 2.0 * noise_amp / HASH_UNIT
PULL = friction / FORCE_UNIT
HEAT_UNIT = 0.5 * friction / (PULL * PULL)
WARM = conductivity / HEAT_UNIT
STRENGTH = 0.5 / FORCE_UNIT
STRENGTH_SHIFT = -0.5 / MODULUS * HASH_UNIT

GROUP_ROWS = 8
K_WIDE = 64
K_SLIM = 32


def round_up(value, multiple):
    return (value + multiple - 1) // multiple * multiple


def parts_of(value):
    high = value.astype(BF16).astype(F32)
    rest = value - high
    middle = rest.astype(BF16).astype(F32)
    low = (rest - middle).astype(BF16).astype(F32)
    return high, middle, low


def bead_terms(raw):
    shape = raw.shape
    row = lax.broadcasted_iota(I32, shape, 1)
    position = row < 3
    scale = jnp.where(row < 6, 1.0, jnp.where(row == 6, WARM, STRENGTH)).astype(F32)
    shift = jnp.where(position, -MIDDLE, jnp.where(row == 7, STRENGTH_SHIFT, 0.0)).astype(F32)
    base = raw * scale + shift
    high, middle, low = parts_of(base)
    swapped = jnp.concatenate([base[:, 3:6], base[:, 0:3], jnp.zeros_like(base[:, 0:2])], 1)
    square = jnp.sum(jnp.where(position, base * base, 0.0), 1, keepdims=True) + 0.005
    cross = PULL * jnp.sum(jnp.where(position, base * swapped, 0.0), 1, keepdims=True)
    return row, base, (high, middle, low), swapped, parts_of(square), parts_of(cross)


def rows_of(row, values, first=0):
    out = jnp.zeros(row.shape, F32)
    for at, value in enumerate(values):
        out = jnp.where(row == first + at, value, out)
    return out


def tall_rows(terms):
    row, _, (high, middle, low), _, square, cross = terms
    ones = jnp.ones(row.shape, F32)
    own = rows_of(row, square + cross)
    return jnp.concatenate([high, middle, low, ones, high, high, middle, own], 1)


def wide_rows(terms):
    row, base, (high, middle, low), swapped, square, cross = terms
    near = [jnp.where(row < 3, -2.0 * part, 0.0) for part in (high, middle, low)]
    pull = parts_of(-PULL * swapped)
    one_square = jnp.where(row < 3, 1.0, 0.0).astype(F32)
    one_cross = jnp.where((row >= 3) & (row < 6), 1.0, 0.0).astype(F32)

    def stack(part, theirs, one):
        return jnp.concatenate([part[0]] * 3 + [theirs, part[1], part[2], part[1], one], 1)

    wide = jnp.concatenate(
        [stack(near, rows_of(row, square), one_square), stack(pull, rows_of(row, cross), one_cross)], 2
    )
    one_strength = jnp.where(row == 7, 1.0, 0.0).astype(F32)
    one_warm = jnp.where(row == 6, -1.0, 0.0).astype(F32)
    strengths = rows_of(row, [part[:, 7:8] for part in (high, middle, low)])
    warmths = rows_of(row, [part[:, 6:7] for part in (high, middle, low)])
    slim = jnp.concatenate(
        [
            jnp.concatenate([one_strength] * 3 + [strengths], 1),
            jnp.concatenate([one_warm] * 3 + [warmths], 1),
        ],
        2,
    )
    return wide.astype(BF16), slim.astype(BF16)


def weigh_rows(terms):
    row, _, (high, middle, low), _, _, _ = terms
    second = rows_of(row, [middle[:, at : at + 1] for at in range(3)] + [low[:, at : at + 1] for at in range(3)] + [1.0])
    return jnp.concatenate([high, second], 1).astype(BF16)


def hash_rows(keys):
    whole = int(HASH_UNIT) // MODULUS
    left = int(HASH_UNIT) - whole * MODULUS
    seed = keys + 1.0
    extra = jnp.floor(seed * (left / MODULUS) + 0.5)
    return seed.astype(I32), seed.astype(I32) * whole + extra.astype(I32)


def interactions(tall, wide, slim, seeds, factors):
    first = jnp.dot(tall, wide, preferred_element_type=F32)
    second = jnp.dot(tall[:, :K_SLIM], slim, preferred_element_type=F32)
    radius2, pull = first[:, :128], first[:, 128:]
    strength, warmth = second[:, :128], second[:, 128:]
    turned = seeds * factors + jnp.int32(-(2**31))
    lift = jnp.maximum(lax.rsqrt(radius2) - 1.0, 0.0)
    drag = lift * pull
    gain = lift * (strength + turned.astype(F32) - drag)
    viscous = drag * drag
    conduct = lift * lift * radius2 * warmth
    return gain, viscous + conduct, viscous - conduct


def halves(value):
    high = value.astype(BF16)
    return high, (value - high.astype(F32)).astype(BF16)


def gather_kernel(
    n_grp, n_tile, cap, blocks, places_ref, coords_ref, speeds_ref, temp_ref, strength_ref, keys_ref,
    held_ref, own, box, far_box, send_sems, recv_sems, up_sems, down_sems, near_box,
):
    g, t = lax.axis_index("grp"), lax.axis_index("tile")
    above, below = lax.rem(g + 1, n_grp), lax.rem(g + n_grp - 1, n_grp)
    barrier = pltpu.get_barrier_semaphore()
    for step in range(1, n_tile):
        pl.semaphore_signal(barrier, inc=1, device_id=(g, lax.rem(t + step, n_tile)), device_id_type=MESH)
    pl.semaphore_signal(barrier, inc=1, device_id=(below, t), device_id_type=MESH)

    def pack(b, carry):
        lanes = pl.ds(pl.multiple_of(b * 128, 128), 128)
        own[b, 0:3] = coords_ref[:, lanes]
        own[b, 3:6] = speeds_ref[:, lanes]
        own[b, 6:7] = temp_ref[pl.ds(b, 1)]
        own[b, 7:8] = strength_ref[pl.ds(b, 1)]
        own[b, 8:9] = keys_ref[pl.ds(b, 1)].astype(F32)
        return carry

    lax.fori_loop(0, blocks, pack, 0, unroll=8)

    def fill(worker):
        for c in range(cap):
            place = places_ref[worker * cap + c]
            box[worker, 8 * c : 8 * c + 8] = own[place, 0:8]
            box[worker, 8 * cap + c : 8 * cap + c + 1] = own[place, 8:9]

    def outgoing(step):
        worker = lax.rem(t + step, n_tile)
        return pltpu.make_async_remote_copy(
            src_ref=box.at[worker], dst_ref=near_box.at[t], send_sem=send_sems.at[step], recv_sem=recv_sems.at[t],
            device_id=(g, worker), device_id_type=MESH,
        )

    def incoming(owner):
        return pltpu.make_async_remote_copy(
            src_ref=box.at[owner], dst_ref=near_box.at[owner], send_sem=send_sems.at[0], recv_sem=recv_sems.at[owner],
            device_id=(g, owner), device_id_type=MESH,
        )

    def upward(owner, source):
        return pltpu.make_async_remote_copy(
            src_ref=source.at[owner], dst_ref=far_box.at[owner], send_sem=up_sems.at[owner], recv_sem=down_sems.at[owner],
            device_id=(above, t), device_id_type=MESH,
        )

    pl.semaphore_wait(barrier, n_tile)

    def send(step, carry):
        fill(lax.rem(t + step, n_tile))
        outgoing(step).start()
        return carry

    lax.fori_loop(1, n_tile, send, 0)
    fill(t)
    near_box[t] = box[t]
    upward(t, near_box).start()

    def take(step, carry):
        owner = lax.rem(t + n_tile - step, n_tile)
        incoming(owner).wait_recv()
        upward(owner, near_box).start()
        return carry

    lax.fori_loop(1, n_tile, take, 0)
    held_ref[0:n_tile] = near_box[...]

    def finish(owner, carry):
        copy = upward(owner, near_box)
        copy.wait_send()
        copy.wait_recv()
        return carry

    lax.fori_loop(0, n_tile, finish, 0)

    def sent(step, carry):
        outgoing(step).wait_send()
        return carry

    lax.fori_loop(1, n_tile, sent, 0)
    held_ref[n_tile:] = far_box[...]


def gather_blocks(n_grp, n_tile, cap, blocks, places, coords, speeds, temp, strength, keys):
    rows = round_up(9 * cap, 8)
    box = pltpu.VMEM((n_tile, rows, 128), F32)
    sems = pltpu.SemaphoreType.DMA((n_tile,))
    vmem = pl.BlockSpec(memory_space=pltpu.VMEM)
    return pl.pallas_call(
        functools.partial(gather_kernel, n_grp, n_tile, cap, blocks),
        out_shape=jax.ShapeDtypeStruct((2 * n_tile, rows, 128), F32),
        in_specs=[pl.BlockSpec(memory_space=pltpu.SMEM)] + [vmem] * 5,
        out_specs=vmem,
        scratch_shapes=[pltpu.VMEM((blocks, 16, 128), F32), box, box, sems, sems, sems, sems, box],
        compiler_params=pltpu.CompilerParams(collective_id=0, has_side_effects=True, vmem_limit_bytes=24 * MIB),
        name="gather_blocks",
    )(places, coords, speeds, temp, strength, keys)


def self_kernel(blocks, coords_ref, speeds_ref, temp_ref, strength_ref, keys_ref, out_ref):
    def step(b, carry):
        lanes = pl.ds(pl.multiple_of(b * 128, 128), 128)
        raw = jnp.concatenate(
            [coords_ref[:, lanes], speeds_ref[:, lanes], temp_ref[pl.ds(b, 1)], strength_ref[pl.ds(b, 1)]], 0
        )[None]
        seed, factor = hash_rows(keys_ref[pl.ds(b, 1)].astype(F32))
        terms = bead_terms(raw)
        wide, slim = wide_rows(terms)
        stack = jnp.concatenate([tall_rows(terms)[0], jnp.broadcast_to(seed.astype(F32), (64, 128))], 0).T
        tall = stack[:, :K_WIDE].astype(BF16)
        seeds = jnp.broadcast_to(stack[:, K_WIDE : K_WIDE + 1].astype(I32), (128, 128))
        gain, _, heat = interactions(tall, wide[0], slim[0], seeds, factor)
        high, low = halves(gain)
        weigh = weigh_rows(terms)[0]
        sums = jnp.dot(
            jnp.concatenate([weigh, weigh], 1), jnp.concatenate([high, low], 0), preferred_element_type=F32
        )
        out_ref[b] = result_rows(terms[1][0], sums, jnp.sum(heat, 0, keepdims=True))
        return carry

    lax.fori_loop(0, blocks, step, 0, unroll=2)


def result_rows(base, sums, heat):
    moved = sums[0:3] + sums[8:11] + sums[11:14]
    force = FORCE_UNIT * (base[0:3] * sums[14:15] - moved)
    return jnp.concatenate([force, HEAT_UNIT * heat], 0)


def self_terms(blocks, coords, speeds, temp, strength, keys):
    vmem = pl.BlockSpec(memory_space=pltpu.VMEM)
    return pl.pallas_call(
        functools.partial(self_kernel, blocks),
        out_shape=jax.ShapeDtypeStruct((blocks, 4, 128), F32),
        in_specs=[vmem] * 5,
        out_specs=vmem,
        compiler_params=pltpu.CompilerParams(vmem_limit_bytes=24 * MIB),
        name="self_terms",
    )(coords, speeds, temp, strength, keys)


GANG = 8


def pair_kernel(
    n_tile, cap, pairs_ref, live_ref, held_ref, out_ref,
    tall_s, wide_s, slim_s, weigh_s, seeds_s, factor_s, acc, heat_acc,
):
    slots = n_tile * cap

    def prepare(owner, first, with_tall):
        boxed = held_ref.at[owner]
        raw = boxed[0 : 8 * cap].reshape(cap, 8, 128)
        seed, factor = hash_rows(boxed[8 * cap : 9 * cap])
        for c in range(0, cap, 4):
            slot = first + c
            terms = bead_terms(raw[c : c + 4])
            wide, slim = wide_rows(terms)
            wide_s[pl.ds(slot, 4)] = wide
            slim_s[pl.ds(slot, 4)] = slim
            weigh_s[pl.ds(slot, 4)] = weigh_rows(terms)
            acc[pl.ds(slot, 4)] = jnp.zeros((4, 24, 128), F32)
            for n in range(4):
                factor_s[slot + n] = factor[c + n : c + n + 1]
            if with_tall:
                tall = tall_rows(terms)
                for n in range(4):
                    mine = jnp.broadcast_to(seed[c + n : c + n + 1].astype(F32), (64, 128))
                    stack = jnp.concatenate([tall[n], mine], 0).T
                    tall_s[slot + n] = stack[:, :K_WIDE].astype(BF16)
                    seeds_s[slot + n] = jnp.broadcast_to(stack[:, K_WIDE : K_WIDE + 1].astype(I32), (128, 128))
                    heat_acc[slot + n] = jnp.zeros((128, 128), F32)

    def near_step(owner, carry):
        prepare(owner, owner * cap, True)
        return carry

    def far_step(owner, carry):
        prepare(n_tile + owner, slots + owner * cap, False)
        return carry

    lax.fori_loop(0, n_tile, near_step, 0)
    lax.fori_loop(0, n_tile, far_step, 0)

    live = live_ref[0]

    def gang(step, carry):
        firsts, seconds, results = [], [], []
        for u in range(GANG):
            k = step * GANG + u
            dead = k >= live
            p, q = pairs_ref[2 * k], pairs_ref[2 * k + 1]
            gain, heat_p, heat_q = interactions(tall_s[p], wide_s[q], slim_s[q], seeds_s[p], factor_s[q])
            firsts.append((p, jnp.where(dead, slots, p)))
            seconds.append((q, jnp.where(dead, 2 * slots, q)))
            results.append((halves(gain), heat_p, jnp.sum(heat_q.reshape(16, 8, 128), 0)))
        for u in range(0, GANG, 2):
            (h0, l0), (h1, l1) = results[u][0], results[u + 1][0]
            weigh_p = [weigh_s[firsts[v][0]] for v in (u, u + 1)]
            weigh_q = [weigh_s[seconds[v][0]] for v in (u, u + 1)]
            down = jnp.concatenate([jnp.concatenate([h0, h1], 1), jnp.concatenate([l0, l1], 1)], 0)
            across = jnp.concatenate([jnp.concatenate([h0, l0], 1), jnp.concatenate([h1, l1], 1)], 0)
            left = jnp.concatenate([jnp.concatenate([w, w], 1) for w in weigh_p], 0)
            right = jnp.concatenate([jnp.concatenate([w, w], 1) for w in weigh_q], 0)
            on_q = jnp.dot(left, down, preferred_element_type=F32)
            on_p = lax.dot_general(right, across, (((1,), (1,)), ((), ())), preferred_element_type=F32)
            for v in (0, 1):
                rows, lanes = slice(16 * v, 16 * v + 16), slice(128 * v, 128 * v + 128)
                to_p, to_q = firsts[u + v][1], seconds[u + v][1]
                acc_p = jnp.where(to_p == slots, 2 * slots, to_p)
                acc[acc_p, 0:16] += on_p[rows, lanes]
                acc[to_q, 0:16] += on_q[rows, lanes]
                acc[to_q, 16:24] += results[u + v][2]
                heat_acc[to_p] += results[u + v][1]
        return carry

    lax.fori_loop(0, lax.div(live + GANG - 1, GANG), gang, 0)

    ones = jnp.ones((16, 256), BF16)

    def near_out(owner, carry):
        boxed = held_ref.at[owner]
        for c in range(0, cap, 2):
            rows = []
            for n in (0, 1):
                rows.append(jnp.concatenate(halves(heat_acc[owner * cap + c + n]), 1))
            heats = lax.dot_general(
                ones, jnp.concatenate(rows, 0), (((1,), (1,)), ((), ())), preferred_element_type=F32
            )
            for n in (0, 1):
                slot = owner * cap + c + n
                sums = acc[slot]
                heat = jnp.sum(sums[16:24], 0, keepdims=True) + heats[0:1, 128 * n : 128 * n + 128]
                base = boxed[8 * (c + n) : 8 * (c + n) + 8] - MIDDLE
                out_ref[owner, 4 * (c + n) : 4 * (c + n) + 4] = result_rows(base, sums, heat)
        return carry

    def far_out(owner, carry):
        boxed = held_ref.at[n_tile + owner]
        for c in range(cap):
            sums = acc[slots + owner * cap + c]
            heat = jnp.sum(sums[16:24], 0, keepdims=True)
            base = boxed[8 * c : 8 * c + 8] - MIDDLE
            out_ref[n_tile + owner, 4 * c : 4 * c + 4] = result_rows(base, sums, heat)
        return carry

    lax.fori_loop(0, n_tile, near_out, 0)
    lax.fori_loop(0, n_tile, far_out, 0)


def pair_terms(n_tile, cap, pairs, live, held):
    slots = n_tile * cap
    smem = pl.BlockSpec(memory_space=pltpu.SMEM)
    vmem = pl.BlockSpec(memory_space=pltpu.VMEM)
    return pl.pallas_call(
        functools.partial(pair_kernel, n_tile, cap),
        out_shape=jax.ShapeDtypeStruct((2 * n_tile, 4 * cap, 128), F32),
        in_specs=[smem, smem, vmem],
        out_specs=vmem,
        scratch_shapes=[
            pltpu.VMEM((slots, 128, K_WIDE), BF16),
            pltpu.VMEM((2 * slots, K_WIDE, 256), BF16),
            pltpu.VMEM((2 * slots, K_SLIM, 256), BF16),
            pltpu.VMEM((2 * slots, 16, 128), BF16),
            pltpu.VMEM((slots, 128, 128), I32),
            pltpu.VMEM((2 * slots, 1, 128), I32),
            pltpu.VMEM((2 * slots + 1, 24, 128), F32),
            pltpu.VMEM((slots + 1, 128, 128), F32),
        ],
        compiler_params=pltpu.CompilerParams(vmem_limit_bytes=63 * MIB),
        name="pair_terms",
    )(pairs, live, held)


def return_kernel(n_grp, n_tile, terms_ref, got_ref, box, send_sems, recv_sems):
    g, t = lax.axis_index("grp"), lax.axis_index("tile")
    above, below = lax.rem(g + 1, n_grp), lax.rem(g + n_grp - 1, n_grp)
    barrier = pltpu.get_barrier_semaphore()
    for step in range(n_tile):
        owner = lax.rem(t + step, n_tile)
        if step:
            pl.semaphore_signal(barrier, inc=1, device_id=(g, owner), device_id_type=MESH)
        pl.semaphore_signal(barrier, inc=1, device_id=(above, owner), device_id_type=MESH)
    pl.semaphore_wait(barrier, 2 * n_tile - 1)

    def near(owner, slot):
        return pltpu.make_async_remote_copy(
            src_ref=terms_ref.at[owner], dst_ref=box.at[slot], send_sem=send_sems.at[owner], recv_sem=recv_sems.at[slot],
            device_id=(g, owner), device_id_type=MESH,
        )

    def far(owner, slot):
        return pltpu.make_async_remote_copy(
            src_ref=terms_ref.at[n_tile + owner], dst_ref=box.at[n_tile + slot], send_sem=send_sems.at[n_tile + owner],
            recv_sem=recv_sems.at[n_tile + slot], device_id=(below, owner), device_id_type=MESH,
        )

    def start(step, carry):
        owner = lax.rem(t + step, n_tile)
        far(owner, t).start()
        near(owner, t).start()
        return carry

    far(t, t).start()
    lax.fori_loop(1, n_tile, start, 0)
    box[t] = terms_ref[t]
    far(t, t).wait()

    def finish(step, carry):
        other = lax.rem(t + step, n_tile)
        far(other, other).wait_send()
        near(other, other).wait_send()
        far(other, other).wait_recv()
        near(other, other).wait_recv()
        return carry

    lax.fori_loop(1, n_tile, finish, 0)
    got_ref[...] = box[...]


def return_terms(n_grp, n_tile, terms):
    vmem = pl.BlockSpec(memory_space=pltpu.VMEM)
    sems = pltpu.SemaphoreType.DMA((2 * n_tile,))
    return pl.pallas_call(
        functools.partial(return_kernel, n_grp, n_tile),
        out_shape=jax.ShapeDtypeStruct(terms.shape, F32),
        in_specs=[vmem],
        out_specs=vmem,
        scratch_shapes=[pltpu.VMEM(terms.shape, F32), sems, sems],
        compiler_params=pltpu.CompilerParams(collective_id=1, has_side_effects=True, vmem_limit_bytes=24 * MIB),
        name="return_terms",
    )(terms)


def total_kernel(n_tile, cap, blocks, places_ref, got_ref, self_ref, out_ref, acc):
    acc[...] = self_ref[...]

    def add(worker, carry):
        for c in range(cap):
            place = places_ref[worker * cap + c]
            rows = slice(4 * c, 4 * c + 4)
            acc[place] += got_ref[worker, rows] + got_ref[n_tile + worker, rows]
        return carry

    lax.fori_loop(0, n_tile, add, 0)

    def put(b, carry):
        out_ref[:, pl.ds(pl.multiple_of(b * 128, 128), 128)] = acc[b]
        return carry

    lax.fori_loop(0, blocks, put, 0, unroll=8)


def total_terms(n_tile, cap, blocks, places, got, selfs):
    smem = pl.BlockSpec(memory_space=pltpu.SMEM)
    vmem = pl.BlockSpec(memory_space=pltpu.VMEM)
    return pl.pallas_call(
        functools.partial(total_kernel, n_tile, cap, blocks),
        out_shape=jax.ShapeDtypeStruct((4, blocks * 128), F32),
        in_specs=[smem, vmem, vmem],
        out_specs=vmem,
        scratch_shapes=[pltpu.VMEM((blocks, 4, 128), F32)],
        compiler_params=pltpu.CompilerParams(vmem_limit_bytes=24 * MIB),
        name="total_terms",
    )(places, got, selfs)


def per_device(
    molecule_coords,
    molecule_speeds,
    molecule_thermal_state,
    conservative_strength,
    noise_keys,
    exported_tile_places,
    tile_couplings,
    processor_coupling_tally,
):
    n_grp, n_tile = lax.axis_size("grp"), lax.axis_size("tile")
    blocks = molecule_coords.shape[1] // 128
    cap = exported_tile_places.shape[2]
    places = exported_tile_places.reshape(-1)
    beads = (
        molecule_coords,
        molecule_speeds,
        molecule_thermal_state.reshape(blocks, 128),
        conservative_strength.reshape(blocks, 128),
        noise_keys.reshape(blocks, 128),
    )
    pairs = jnp.pad(tile_couplings.reshape(-1), (0, 2 * GANG))
    held = gather_blocks(n_grp, n_tile, cap, blocks, places, *beads)
    selfs = self_terms(blocks, *beads)
    terms = pair_terms(n_tile, cap, pairs, processor_coupling_tally, held)
    got = return_terms(n_grp, n_tile, terms)
    return total_terms(n_tile, cap, blocks, places, got, selfs)


def solution(mesh):
    in_specs = (
        P(None, ("grp", "tile")),
        P(None, ("grp", "tile")),
        P(("grp", "tile")),
        P(("grp", "tile")),
        P(("grp", "tile")),
        P(("grp", "tile"), None, None),
        P(("grp", "tile"), None, None),
        P(("grp", "tile")),
    )
    out_specs = P(None, ("grp", "tile"))
    return jax.shard_map(per_device, mesh=mesh, in_specs=in_specs, out_specs=out_specs, check_vma=False)
```

time: 836 us -> 205 us (0.25)
  other arithmetic: 564 us -> 0 us
  Pallas kernels: 0 us -> 193 us
  local copies, waits for them, and re-layouts: 123 us -> 8.79 us
  waiting for transfers between devices: 74.5 us -> 0 us
  matrix products: 23.4 us -> 0 us
  blocking collectives: 19.5 us -> 0 us
  between operations: 14.2 us -> 0.78 us
    reduce_sum x88 -> x0, other arithmetic: 516 us -> none  [the longest x16 147 us: tile_pair(): jnp.sum(viscous - conduct, 0)[None]]
    pallas_call x0 -> x5, Pallas kernels: none -> 193 us  [the longest x1 77 us: pair_terms(): pl.pallas_call(functools.partial(pair_kernel, n_tile, cap), out_shape=jax...]
    gather x34 -> x0, local copies, waits for them, and re-layouts: 57.5 us -> none  [the longest x16 39.7 us: consume(): reachable[second_index]]
    all_gather x1 -> x0, waiting for transfers between devices: 54.9 us -> none  [per_device(): group_data = lax.all_gather(owned, 'tile', axis=0, tiled=True)]
    dot_general x33 -> x0, matrix products: 23.4 us -> none  [the longest x16 11.1 us: consume(): jnp.dot(one_hot(second_index, 2 * buffer_len).T, on_second, precision=lax...]
    sqrt x24 -> x0, other arithmetic: 19.5 us -> none  [the longest x16 17.3 us: tile_pair(): radius = jnp.sqrt(jnp.sum(offset * offset, 0) + 0.01)]
    all_gather x1 -> x0, blocking collectives: 19.5 us -> none  [per_device(): tables = lax.all_gather(exported_tile_places, 'tile', axis=0, tiled=True)]
    mul x9 -> x0, other arithmetic: 19.2 us -> none  [the longest x8 19.2 us: tile_self(): (repulse * weight - friction * weight * weight * along + noise_amp * weig...]
  transfers between devices with their start and end apart: 4 -> 0, of which waited for: 4 -> 0; matrix products, arithmetic and copies ran while one was open for 9% -> 0% of each run, Pallas kernels for 0% -> 0%
where the time goes in v1:
time: 205 us; the launch traced here: 203 us
  Pallas kernels  193 us (94%)
  local copies, waits for them, and re-layouts  8.79 us (4%)
    pallas_call x1, Pallas kernels, pair_terms(): pl.pallas_call(functools.partial(pair_kernel, n_tile, cap), out_shape=jax...  77 us
    pallas_call x1, Pallas kernels, return_terms(): pl.pallas_call(functools.partial(return_kernel, n_grp, n_tile), out_shape...  55.1 us
    pallas_call x1, Pallas kernels, self_terms(): pl.pallas_call(functools.partial(self_kernel, blocks), out_shape=jax.Shap...  35.3 us
    pallas_call x1, Pallas kernels, gather_blocks(): pl.pallas_call(functools.partial(gather_kernel, n_grp, n_tile, cap, block...  23.7 us
    unnamed x28, local copies, waits for them, and re-layouts  7.82 us

profile of v1, /device:TPU:99, one launch (start us, length us, event | category | flops | bytes accessed | tf_op | source)
XLA Modules:
  0.0 202.8 jit_solution(9539541145875881033)
XLA Ops:
  0.0 0.0 copy-start.12
  0.0 0.8 copy.9
  0.8 0.1 reshape.15.places_ref
  0.9 0.0 copy-start.2
  0.9 0.9 copy-done.2
  1.8 0.0 copy-start.4
  1.8 0.9 copy-done.4
  2.8 0.0 copy-start.6
  2.8 0.8 copy-done.6
  3.6 0.0 copy-start.8
  3.6 0.8 copy-done.8
  4.5 0.0 copy-start.10
  4.5 0.8 copy-done.10
  5.3 23.7 %gather_blocks.1.held_ref = f32[32,112,128]{2,1,0:T(8,128)S(1)} custom-call(s32[192]{0:T(256)S(1)} %reshape.15.places_ref, f32[3,16384]{1,0:T(4,128)S(1)} %copy-done.2, f32[3,16384]{1,0:T(4,128)S(1)} %copy-done.4, f32[128,128]{1,0:T(8,128)S(1)} %bitcast.3, f32[128,128]{1,0:T(8,128)S(1)} %bitcast.5, s32[128,128]{1,0:T(8,128)S(1)} %bitcast.7), custom_call_target="tpu_custom_call" | custom-call | tf_op jit(solution)/shard_map/gather_blocks/pallas_call | solution.py:224
  29.0 0.0 copy-start
  29.0 1.2 copy-done
  30.3 0.0 copy-done.12
  30.3 0.2 copy.10
  30.5 0.3 reshape.16
  30.8 0.6 pad.4.pairs_ref
  32.0 0.0 copy-start.3
  32.0 0.0 copy-start.5
  32.1 0.0 copy-start.7
  32.1 0.0 copy-start.9
  32.1 0.0 copy-start.11
  32.1 77.0 %pair_terms.1.terms_ref = f32[32,48,128]{2,1,0:T(8,128)} custom-call(s32[2064]{0:T(1024)} %pad.4.pairs_ref, s32[1]{0:T(128)S(6)} %copy.11.live_ref, f32[32,112,128]{2,1,0:T(8,128)} %copy-done), custom_call_target="tpu_custom_call" | custom-call | tf_op jit(solution)/shard_map/pair_terms/pallas_call | solution.py:390
  109.1 0.0 copy-start.1
  109.1 1.1 copy-done.1
  110.3 55.1 %return_terms.1.got_ref = f32[32,48,128]{2,1,0:T(8,128)S(1)} custom-call(f32[32,48,128]{2,1,0:T(8,128)S(1)} %copy-done.1), custom_call_target="tpu_custom_call" | custom-call | tf_op jit(solution)/shard_map/return_terms/pallas_call | solution.py:459
  165.4 0.0 copy-done.3
  165.4 0.0 copy-done.5
  165.4 0.0 copy-done.7
  165.4 0.0 copy-done.9
  165.4 0.0 copy-done.11
  165.4 35.3 %self_terms.1.self_ref = f32[128,4,128]{2,1,0:T(4,128)S(1)} custom-call(f32[3,16384]{1,0:T(4,128)S(1)} %copy-done.3, f32[3,16384]{1,0:T(4,128)S(1)} %copy-done.5, f32[128,128]{1,0:T(8,128)S(1)} %bitcast.4, f32[128,128]{1,0:T(8,128)S(1)} %bitcast.6, s32[128,128]{1,0:T(8,128)S(1)} %bitcast.8), custom_call_target="tpu_custom_call" | custom-call | tf_op jit(solution)/shard_map/self_terms/pallas_call | solution.py:267
  200.7 2.0 %total_terms.1 = f32[4,16384]{1,0:T(4,128)} custom-call(s32[192]{0:T(256)S(1)} %reshape.15.places_ref, f32[32,48,128]{2,1,0:T(8,128)S(1)} %return_terms.1.got_ref, f32[128,4,128]{2,1,0:T(4,128)S(1)} %self_terms.1.self_ref), custom_call_target="tpu_custom_call" | custom-call | tf_op jit(solution)/shard_map/total_terms/pallas_call | solution.py:492
Async XLA Ops:
  0.0 30.3 %copy-start.12 = (s32[1,1024,2]{1,2,0:T(2,128)S(1)}, s32[1,1024,2]{1,2,0:T(2,128)}, u32[]{:S(2)}) copy-start(s32[1,1024,2]{1,2,0:T(2,128)} %param.14) | copy-start | bytes 24580
  0.9 1.0 copy-start.2
  1.8 0.9 copy-start.4
  2.8 0.8 copy-start.6
  3.6 0.8 copy-start.8
  4.5 0.8 copy-start.10
  29.0 1.3 copy-start
  32.0 133.3 %copy-start.3 = (f32[3,16384]{1,0:T(4,128)S(1)}, f32[3,16384]{1,0:T(4,128)}, u32[]{:S(2)}) copy-start(f32[3,16384]{1,0:T(4,128)} %coords_ref.3) | copy-start | bytes 589828
  32.0 133.3 %copy-start.5 = (f32[3,16384]{1,0:T(4,128)S(1)}, f32[3,16384]{1,0:T(4,128)}, u32[]{:S(2)}) copy-start(f32[3,16384]{1,0:T(4,128)} %speeds_ref.3) | copy-start | bytes 589828
  32.1 133.3 %copy-start.7 = (f32[16384]{0:T(1024)S(1)}, f32[16384]{0:T(1024)}, u32[]{:S(2)}) copy-start(f32[16384]{0:T(1024)} %param.10) | copy-start | bytes 196612
  32.1 133.3 %copy-start.9 = (f32[16384]{0:T(1024)S(1)}, f32[16384]{0:T(1024)}, u32[]{:S(2)}) copy-start(f32[16384]{0:T(1024)} %param.11) | copy-start | bytes 196612
  32.1 133.3 %copy-start.11 = (s32[16384]{0:T(1024)S(1)}, s32[16384]{0:T(1024)}, u32[]{:S(2)}) copy-start(s32[16384]{0:T(1024)} %param.12) | copy-start | bytes 196612
  109.1 1.1 copy-start.1

commit v2 on v1

--- a/solution.py
+++ b/solution.py
@@ -114,8 +114,17 @@
 
 
 def interactions(tall, wide, slim, seeds, factors):
+    return finish(products(tall, wide, slim), seeds, factors)
+
+
+def products(tall, wide, slim):
     first = jnp.dot(tall, wide, preferred_element_type=F32)
     second = jnp.dot(tall[:, :K_SLIM], slim, preferred_element_type=F32)
+    return first, second
+
+
+def finish(both, seeds, factors):
+    first, second = both
     radius2, pull = first[:, :128], first[:, 128:]
     strength, warmth = second[:, :128], second[:, 128:]
     turned = seeds * factors + jnp.int32(-(2**31))
@@ -132,16 +141,68 @@
     return high, (value - high.astype(F32)).astype(BF16)
 
 
+SELF_GANG = 4
+
+
+def result_rows(base, sums, heat):
+    moved = sums[0:3] + sums[8:11] + sums[11:14]
+    force = FORCE_UNIT * (base[0:3] * sums[14:15] - moved)
+    return jnp.concatenate([force, HEAT_UNIT * heat], 0)
+
+
+def self_blocks(first, beads, out_ref, at):
+    coords_ref, speeds_ref, temp_ref, strength_ref, keys_ref = beads
+    raws, seeds, factors = [], [], []
+    for n in range(SELF_GANG):
+        b = first + n
+        lanes = pl.ds(pl.multiple_of(b * 128, 128), 128)
+        raws.append(
+            jnp.concatenate(
+                [coords_ref[:, lanes], speeds_ref[:, lanes], temp_ref[pl.ds(b, 1)], strength_ref[pl.ds(b, 1)]], 0
+            )
+        )
+        seed, factor = hash_rows(keys_ref[pl.ds(b, 1)].astype(F32))
+        seeds.append(seed)
+        factors.append(factor)
+    terms = bead_terms(jnp.stack(raws))
+    wide, slim = wide_rows(terms)
+    tall, weigh = tall_rows(terms), weigh_rows(terms)
+    stacks = [
+        jnp.concatenate([tall[n], jnp.broadcast_to(seeds[n].astype(F32), (64, 128))], 0).T for n in range(SELF_GANG)
+    ]
+    both = [products(stacks[n][:, :K_WIDE].astype(BF16), wide[n], slim[n]) for n in range(SELF_GANG)]
+    halved, heats = [], []
+    for n in range(SELF_GANG):
+        mine = jnp.broadcast_to(stacks[n][:, K_WIDE : K_WIDE + 1].astype(I32), (128, 128))
+        gain, _, heat = finish(both[n], mine, factors[n])
+        halved.append(jnp.concatenate(halves(gain), 0))
+        heats.append(jnp.sum(heat, 0, keepdims=True))
+    for n in range(0, SELF_GANG, 2):
+        left = jnp.concatenate([jnp.concatenate([weigh[m], weigh[m]], 1) for m in (n, n + 1)], 0)
+        sums = jnp.dot(left, jnp.concatenate(halved[n : n + 2], 1), preferred_element_type=F32)
+        for m in (0, 1):
+            mine = sums[16 * m : 16 * m + 16, 128 * m : 128 * m + 128]
+            out_ref[at + n + m] = result_rows(terms[1][n + m], mine, heats[n + m])
+
+
 def gather_kernel(
-    n_grp, n_tile, cap, blocks, places_ref, coords_ref, speeds_ref, temp_ref, strength_ref, keys_ref,
-    held_ref, own, box, far_box, send_sems, recv_sems, up_sems, down_sems, near_box,
+    n_grp, n_tile, cap, blocks, places_ref, coords_hbm, speeds_hbm, temp_hbm, strength_hbm, keys_hbm,
+    held_ref, self_ref, own, box, send_sems, recv_sems, up_sems, down_sems, home_sem, bead_sems, *beads,
 ):
+    sources = (coords_hbm, speeds_hbm, temp_hbm, strength_hbm, keys_hbm)
+    loads = [pltpu.make_async_copy(source, beads[n], bead_sems.at[n]) for n, source in enumerate(sources)]
+    for load in loads:
+        load.start()
+    coords_ref, speeds_ref, temp_ref, strength_ref, keys_ref = beads
     g, t = lax.axis_index("grp"), lax.axis_index("tile")
     above, below = lax.rem(g + 1, n_grp), lax.rem(g + n_grp - 1, n_grp)
     barrier = pltpu.get_barrier_semaphore()
     for step in range(1, n_tile):
         pl.semaphore_signal(barrier, inc=1, device_id=(g, lax.rem(t + step, n_tile)), device_id_type=MESH)
     pl.semaphore_signal(barrier, inc=1, device_id=(below, t), device_id_type=MESH)
+
+    for load in loads:
+        load.wait()
 
     def pack(b, carry):
         lanes = pl.ds(pl.multiple_of(b * 128, 128), 128)
@@ -156,26 +217,26 @@
 
     def fill(worker):
         for c in range(cap):
-            place = places_ref[worker * cap + c]
+            place = places_ref[0, c, worker]
             box[worker, 8 * c : 8 * c + 8] = own[place, 0:8]
             box[worker, 8 * cap + c : 8 * cap + c + 1] = own[place, 8:9]
 
     def outgoing(step):
         worker = lax.rem(t + step, n_tile)
         return pltpu.make_async_remote_copy(
-            src_ref=box.at[worker], dst_ref=near_box.at[t], send_sem=send_sems.at[step], recv_sem=recv_sems.at[t],
+            src_ref=box.at[worker], dst_ref=held_ref.at[t], send_sem=send_sems.at[step], recv_sem=recv_sems.at[t],
             device_id=(g, worker), device_id_type=MESH,
         )
 
     def incoming(owner):
         return pltpu.make_async_remote_copy(
-            src_ref=box.at[owner], dst_ref=near_box.at[owner], send_sem=send_sems.at[0], recv_sem=recv_sems.at[owner],
+            src_ref=box.at[owner], dst_ref=held_ref.at[owner], send_sem=send_sems.at[0], recv_sem=recv_sems.at[owner],
             device_id=(g, owner), device_id_type=MESH,
         )
 
     def upward(owner, source):
         return pltpu.make_async_remote_copy(
-            src_ref=source.at[owner], dst_ref=far_box.at[owner], send_sem=up_sems.at[owner], recv_sem=down_sems.at[owner],
+            src_ref=source.at[owner], dst_ref=held_ref.at[n_tile + owner], send_sem=up_sems.at[owner], recv_sem=down_sems.at[owner],
             device_id=(above, t), device_id_type=MESH,
         )
 
@@ -188,20 +249,25 @@
 
     lax.fori_loop(1, n_tile, send, 0)
     fill(t)
-    near_box[t] = box[t]
-    upward(t, near_box).start()
+    home = pltpu.make_async_copy(box.at[t], held_ref.at[t], home_sem)
+    home.start()
+    upward(t, box).start()
 
     def take(step, carry):
         owner = lax.rem(t + n_tile - step, n_tile)
         incoming(owner).wait_recv()
-        upward(owner, near_box).start()
+        upward(owner, held_ref).start()
+        some = (step - 1) * SELF_GANG
+        self_blocks(some, beads, self_ref, some)
         return carry
 
     lax.fori_loop(1, n_tile, take, 0)
-    held_ref[0:n_tile] = near_box[...]
+    last = (n_tile - 1) * SELF_GANG
+    self_blocks(last, beads, self_ref, last)
+    home.wait()
 
     def finish(owner, carry):
-        copy = upward(owner, near_box)
+        copy = upward(owner, held_ref)
         copy.wait_send()
         copy.wait_recv()
         return carry
@@ -213,7 +279,11 @@
         return carry
 
     lax.fori_loop(1, n_tile, sent, 0)
-    held_ref[n_tile:] = far_box[...]
+
+
+def bead_buffers(blocks):
+    wide, flat = pltpu.VMEM((3, blocks * 128), F32), pltpu.VMEM((blocks, 128), F32)
+    return [wide, wide, flat, flat, pltpu.VMEM((blocks, 128), I32)]
 
 
 def gather_blocks(n_grp, n_tile, cap, blocks, places, coords, speeds, temp, strength, keys):
@@ -221,67 +291,43 @@
     box = pltpu.VMEM((n_tile, rows, 128), F32)
     sems = pltpu.SemaphoreType.DMA((n_tile,))
     vmem = pl.BlockSpec(memory_space=pltpu.VMEM)
+    hbm = pl.BlockSpec(memory_space=pltpu.HBM)
     return pl.pallas_call(
         functools.partial(gather_kernel, n_grp, n_tile, cap, blocks),
-        out_shape=jax.ShapeDtypeStruct((2 * n_tile, rows, 128), F32),
-        in_specs=[pl.BlockSpec(memory_space=pltpu.SMEM)] + [vmem] * 5,
-        out_specs=vmem,
-        scratch_shapes=[pltpu.VMEM((blocks, 16, 128), F32), box, box, sems, sems, sems, sems, box],
-        compiler_params=pltpu.CompilerParams(collective_id=0, has_side_effects=True, vmem_limit_bytes=24 * MIB),
+        out_shape=[
+            jax.ShapeDtypeStruct((2 * n_tile, rows, 128), F32),
+            jax.ShapeDtypeStruct((n_tile * SELF_GANG, 4, 128), F32),
+        ],
+        in_specs=[pl.BlockSpec(memory_space=pltpu.SMEM)] + [hbm] * 5,
+        out_specs=[hbm, vmem],
+        scratch_shapes=[
+            pltpu.VMEM((blocks, 16, 128), F32), box, sems, sems, sems, sems, pltpu.SemaphoreType.DMA,
+            pltpu.SemaphoreType.DMA((5,)),
+            *bead_buffers(blocks),
+        ],
+        compiler_params=pltpu.CompilerParams(collective_id=0, has_side_effects=True, vmem_limit_bytes=63 * MIB),
         name="gather_blocks",
     )(places, coords, speeds, temp, strength, keys)
 
 
-def self_kernel(blocks, coords_ref, speeds_ref, temp_ref, strength_ref, keys_ref, out_ref):
-    def step(b, carry):
-        lanes = pl.ds(pl.multiple_of(b * 128, 128), 128)
-        raw = jnp.concatenate(
-            [coords_ref[:, lanes], speeds_ref[:, lanes], temp_ref[pl.ds(b, 1)], strength_ref[pl.ds(b, 1)]], 0
-        )[None]
-        seed, factor = hash_rows(keys_ref[pl.ds(b, 1)].astype(F32))
-        terms = bead_terms(raw)
-        wide, slim = wide_rows(terms)
-        stack = jnp.concatenate([tall_rows(terms)[0], jnp.broadcast_to(seed.astype(F32), (64, 128))], 0).T
-        tall = stack[:, :K_WIDE].astype(BF16)
-        seeds = jnp.broadcast_to(stack[:, K_WIDE : K_WIDE + 1].astype(I32), (128, 128))
-        gain, _, heat = interactions(tall, wide[0], slim[0], seeds, factor)
-        high, low = halves(gain)
-        weigh = weigh_rows(terms)[0]
-        sums = jnp.dot(
-            jnp.concatenate([weigh, weigh], 1), jnp.concatenate([high, low], 0), preferred_element_type=F32
-        )
-        out_ref[b] = result_rows(terms[1][0], sums, jnp.sum(heat, 0, keepdims=True))
-        return carry
-
-    lax.fori_loop(0, blocks, step, 0, unroll=2)
-
-
-def result_rows(base, sums, heat):
-    moved = sums[0:3] + sums[8:11] + sums[11:14]
-    force = FORCE_UNIT * (base[0:3] * sums[14:15] - moved)
-    return jnp.concatenate([force, HEAT_UNIT * heat], 0)
-
-
-def self_terms(blocks, coords, speeds, temp, strength, keys):
-    vmem = pl.BlockSpec(memory_space=pltpu.VMEM)
-    return pl.pallas_call(
-        functools.partial(self_kernel, blocks),
-        out_shape=jax.ShapeDtypeStruct((blocks, 4, 128), F32),
-        in_specs=[vmem] * 5,
-        out_specs=vmem,
-        compiler_params=pltpu.CompilerParams(vmem_limit_bytes=24 * MIB),
-        name="self_terms",
-    )(coords, speeds, temp, strength, keys)
-
-
-GANG = 8
+GANG = 16
+AHEAD = 0
+LAG = 6
+LAG_AT = 0
 
 
 def pair_kernel(
-    n_tile, cap, pairs_ref, live_ref, held_ref, out_ref,
-    tall_s, wide_s, slim_s, weigh_s, seeds_s, factor_s, acc, heat_acc,
+    n_tile, cap, pairs_ref, live_ref, held_hbm, out_ref,
+    held_ref, held_sems, tall_s, wide_s, slim_s, weigh_s, seeds_s, factor_s, acc, heat_acc, *gains,
 ):
     slots = n_tile * cap
+
+    def load(half):
+        some = pl.ds(half * n_tile, n_tile)
+        return pltpu.make_async_copy(held_hbm.at[some], held_ref.at[some], held_sems.at[half])
+
+    load(0).start()
+    load(1).start()
 
     def prepare(owner, first, with_tall):
         boxed = held_ref.at[owner]
@@ -314,42 +360,60 @@
         prepare(n_tile + owner, slots + owner * cap, False)
         return carry
 
+    load(0).wait()
     lax.fori_loop(0, n_tile, near_step, 0)
+    load(1).wait()
     lax.fori_loop(0, n_tile, far_step, 0)
 
     live = live_ref[0]
 
     def gang(step, carry):
-        firsts, seconds, results = [], [], []
-        for u in range(GANG):
+        made = {}
+
+        def place(u):
             k = step * GANG + u
-            dead = k >= live
-            p, q = pairs_ref[2 * k], pairs_ref[2 * k + 1]
-            gain, heat_p, heat_q = interactions(tall_s[p], wide_s[q], slim_s[q], seeds_s[p], factor_s[q])
-            firsts.append((p, jnp.where(dead, slots, p)))
-            seconds.append((q, jnp.where(dead, 2 * slots, q)))
-            results.append((halves(gain), heat_p, jnp.sum(heat_q.reshape(16, 8, 128), 0)))
-        for u in range(0, GANG, 2):
-            (h0, l0), (h1, l1) = results[u][0], results[u + 1][0]
-            weigh_p = [weigh_s[firsts[v][0]] for v in (u, u + 1)]
-            weigh_q = [weigh_s[seconds[v][0]] for v in (u, u + 1)]
-            down = jnp.concatenate([jnp.concatenate([h0, h1], 1), jnp.concatenate([l0, l1], 1)], 0)
-            across = jnp.concatenate([jnp.concatenate([h0, l0], 1), jnp.concatenate([h1, l1], 1)], 0)
+            at = jnp.minimum(jnp.maximum(k, 0) if u < 0 else k, pairs_ref.shape[2] - 1)
+            return pairs_ref[0, 0, at], pairs_ref[0, 1, at], ((k >= live) | (k < 0)) if u < 0 else (k >= live)
+
+        def multiply(u):
+            p, q, _ = place(u)
+            made[u] = products(tall_s[p], wide_s[q], slim_s[q])
+
+        def evaluate(u):
+            p, q, dead = place(u)
+            gain, heat_p, heat_q = finish(made.pop(u), seeds_s[p], factor_s[q])
+            heat_acc[jnp.where(dead, slots, p)] += heat_p
+            acc[jnp.where(dead, 2 * slots, q), 16:24] += jnp.sum(heat_q.reshape(16, 8, 128), 0)
+            gains[u % GANG][0:128], gains[u % GANG][128:256] = halves(gain)
+
+        def reduce(u):
+            here = [place(v) for v in (u, u + 1)]
+            first, second = gains[u % GANG], gains[(u + 1) % GANG]
+            weigh_p = [weigh_s[p] for p, _, _ in here]
+            weigh_q = [weigh_s[q] for _, q, _ in here]
+            down = jnp.concatenate([first[...], second[...]], 1)
+            across = jnp.concatenate(
+                [jnp.concatenate([ref[0:128], ref[128:256]], 1) for ref in (first, second)], 0
+            )
             left = jnp.concatenate([jnp.concatenate([w, w], 1) for w in weigh_p], 0)
             right = jnp.concatenate([jnp.concatenate([w, w], 1) for w in weigh_q], 0)
             on_q = jnp.dot(left, down, preferred_element_type=F32)
             on_p = lax.dot_general(right, across, (((1,), (1,)), ((), ())), preferred_element_type=F32)
-            for v in (0, 1):
+            for v, (p, q, dead) in enumerate(here):
                 rows, lanes = slice(16 * v, 16 * v + 16), slice(128 * v, 128 * v + 128)
-                to_p, to_q = firsts[u + v][1], seconds[u + v][1]
-                acc_p = jnp.where(to_p == slots, 2 * slots, to_p)
-                acc[acc_p, 0:16] += on_p[rows, lanes]
-                acc[to_q, 0:16] += on_q[rows, lanes]
-                acc[to_q, 16:24] += results[u + v][2]
-                heat_acc[to_p] += results[u + v][1]
-        return carry
-
-    lax.fori_loop(0, lax.div(live + GANG - 1, GANG), gang, 0)
+                acc[jnp.where(dead, 2 * slots, p), 0:16] += on_p[rows, lanes]
+                acc[jnp.where(dead, 2 * slots, q), 0:16] += on_q[rows, lanes]
+
+        for u in range(-AHEAD, GANG):
+            if 0 <= u + AHEAD < GANG:
+                multiply(u + AHEAD)
+            if u >= 0:
+                evaluate(u)
+                if u % 2 == LAG_AT:
+                    reduce(u - LAG_AT - LAG)
+        return carry
+
+    lax.fori_loop(0, lax.div(live + LAG + GANG - 1, GANG), gang, 0)
 
     ones = jnp.ones((16, 256), BF16)
 
@@ -387,12 +451,15 @@
     slots = n_tile * cap
     smem = pl.BlockSpec(memory_space=pltpu.SMEM)
     vmem = pl.BlockSpec(memory_space=pltpu.VMEM)
+    hbm = pl.BlockSpec(memory_space=pltpu.HBM)
     return pl.pallas_call(
         functools.partial(pair_kernel, n_tile, cap),
         out_shape=jax.ShapeDtypeStruct((2 * n_tile, 4 * cap, 128), F32),
-        in_specs=[smem, smem, vmem],
+        in_specs=[smem, smem, hbm],
         out_specs=vmem,
         scratch_shapes=[
+            pltpu.VMEM(held.shape, F32),
+            pltpu.SemaphoreType.DMA((2,)),
             pltpu.VMEM((slots, 128, K_WIDE), BF16),
             pltpu.VMEM((2 * slots, K_WIDE, 256), BF16),
             pltpu.VMEM((2 * slots, K_SLIM, 256), BF16),
@@ -401,13 +468,21 @@
             pltpu.VMEM((2 * slots, 1, 128), I32),
             pltpu.VMEM((2 * slots + 1, 24, 128), F32),
             pltpu.VMEM((slots + 1, 128, 128), F32),
+            *[pltpu.VMEM((256, 128), BF16)] * GANG,
         ],
         compiler_params=pltpu.CompilerParams(vmem_limit_bytes=63 * MIB),
         name="pair_terms",
     )(pairs, live, held)
 
 
-def return_kernel(n_grp, n_tile, terms_ref, got_ref, box, send_sems, recv_sems):
+def return_kernel(
+    n_grp, n_tile, blocks, terms_ref, coords_hbm, speeds_hbm, temp_hbm, strength_hbm, keys_hbm,
+    got_ref, self_ref, send_sems, recv_sems, home_sem, bead_sems, *beads,
+):
+    sources = (coords_hbm, speeds_hbm, temp_hbm, strength_hbm, keys_hbm)
+    loads = [pltpu.make_async_copy(source, beads[n], bead_sems.at[n]) for n, source in enumerate(sources)]
+    for load in loads:
+        load.start()
     g, t = lax.axis_index("grp"), lax.axis_index("tile")
     above, below = lax.rem(g + 1, n_grp), lax.rem(g + n_grp - 1, n_grp)
     barrier = pltpu.get_barrier_semaphore()
@@ -420,13 +495,13 @@
 
     def near(owner, slot):
         return pltpu.make_async_remote_copy(
-            src_ref=terms_ref.at[owner], dst_ref=box.at[slot], send_sem=send_sems.at[owner], recv_sem=recv_sems.at[slot],
+            src_ref=terms_ref.at[owner], dst_ref=got_ref.at[slot], send_sem=send_sems.at[owner], recv_sem=recv_sems.at[slot],
             device_id=(g, owner), device_id_type=MESH,
         )
 
     def far(owner, slot):
         return pltpu.make_async_remote_copy(
-            src_ref=terms_ref.at[n_tile + owner], dst_ref=box.at[n_tile + slot], send_sem=send_sems.at[n_tile + owner],
+            src_ref=terms_ref.at[n_tile + owner], dst_ref=got_ref.at[n_tile + slot], send_sem=send_sems.at[n_tile + owner],
             recv_sem=recv_sems.at[n_tile + slot], device_id=(below, owner), device_id_type=MESH,
         )
 
@@ -438,7 +513,18 @@
 
     far(t, t).start()
     lax.fori_loop(1, n_tile, start, 0)
-    box[t] = terms_ref[t]
+    home = pltpu.make_async_copy(terms_ref.at[t], got_ref.at[t], home_sem)
+    home.start()
+    for load in loads:
+        load.wait()
+    done = n_tile * SELF_GANG
+
+    def selfs(step, carry):
+        self_blocks(done + step * SELF_GANG, beads, self_ref, step * SELF_GANG)
+        return carry
+
+    lax.fori_loop(0, (blocks - done) // SELF_GANG, selfs, 0)
+    home.wait()
     far(t, t).wait()
 
     def finish(step, carry):
@@ -450,29 +536,37 @@
         return carry
 
     lax.fori_loop(1, n_tile, finish, 0)
-    got_ref[...] = box[...]
-
-
-def return_terms(n_grp, n_tile, terms):
+
+
+def return_terms(n_grp, n_tile, blocks, terms, beads):
     vmem = pl.BlockSpec(memory_space=pltpu.VMEM)
+    hbm = pl.BlockSpec(memory_space=pltpu.HBM)
     sems = pltpu.SemaphoreType.DMA((2 * n_tile,))
     return pl.pallas_call(
-        functools.partial(return_kernel, n_grp, n_tile),
-        out_shape=jax.ShapeDtypeStruct(terms.shape, F32),
-        in_specs=[vmem],
-        out_specs=vmem,
-        scratch_shapes=[pltpu.VMEM(terms.shape, F32), sems, sems],
-        compiler_params=pltpu.CompilerParams(collective_id=1, has_side_effects=True, vmem_limit_bytes=24 * MIB),
+        functools.partial(return_kernel, n_grp, n_tile, blocks),
+        out_shape=[
+            jax.ShapeDtypeStruct(terms.shape, F32),
+            jax.ShapeDtypeStruct((blocks - n_tile * SELF_GANG, 4, 128), F32),
+        ],
+        in_specs=[hbm] * 6,
+        out_specs=[vmem, vmem],
+        scratch_shapes=[
+            sems, sems, pltpu.SemaphoreType.DMA, pltpu.SemaphoreType.DMA((5,)),
+            *bead_buffers(blocks),
+        ],
+        compiler_params=pltpu.CompilerParams(collective_id=1, has_side_effects=True, vmem_limit_bytes=63 * MIB),
         name="return_terms",
-    )(terms)
-
-
-def total_kernel(n_tile, cap, blocks, places_ref, got_ref, self_ref, out_ref, acc):
-    acc[...] = self_ref[...]
+    )(terms, *beads)
+
+
+def total_kernel(n_tile, cap, blocks, places_ref, got_ref, early_ref, late_ref, out_ref, acc):
+    early = early_ref.shape[0]
+    acc[0:early] = early_ref[...]
+    acc[early:blocks] = late_ref[...]
 
     def add(worker, carry):
         for c in range(cap):
-            place = places_ref[worker * cap + c]
+            place = places_ref[0, c, worker]
             rows = slice(4 * c, 4 * c + 4)
             acc[place] += got_ref[worker, rows] + got_ref[n_tile + worker, rows]
         return carry
@@ -486,18 +580,19 @@
     lax.fori_loop(0, blocks, put, 0, unroll=8)
 
 
-def total_terms(n_tile, cap, blocks, places, got, selfs):
+def total_terms(n_tile, cap, blocks, places, got, early, late):
     smem = pl.BlockSpec(memory_space=pltpu.SMEM)
     vmem = pl.BlockSpec(memory_space=pltpu.VMEM)
+    hbm = pl.BlockSpec(memory_space=pltpu.HBM)
     return pl.pallas_call(
         functools.partial(total_kernel, n_tile, cap, blocks),
         out_shape=jax.ShapeDtypeStruct((4, blocks * 128), F32),
-        in_specs=[smem, vmem, vmem],
+        in_specs=[smem, vmem, vmem, vmem],
         out_specs=vmem,
         scratch_shapes=[pltpu.VMEM((blocks, 4, 128), F32)],
-        compiler_params=pltpu.CompilerParams(vmem_limit_bytes=24 * MIB),
+        compiler_params=pltpu.CompilerParams(vmem_limit_bytes=63 * MIB),
         name="total_terms",
-    )(places, got, selfs)
+    )(places, got, early, late)
 
 
 def per_device(
@@ -513,7 +608,7 @@
     n_grp, n_tile = lax.axis_size("grp"), lax.axis_size("tile")
     blocks = molecule_coords.shape[1] // 128
     cap = exported_tile_places.shape[2]
-    places = exported_tile_places.reshape(-1)
+    places = exported_tile_places.transpose(0, 2, 1)
     beads = (
         molecule_coords,
         molecule_speeds,
@@ -521,12 +616,11 @@
         conservative_strength.reshape(blocks, 128),
         noise_keys.reshape(blocks, 128),
     )
-    pairs = jnp.pad(tile_couplings.reshape(-1), (0, 2 * GANG))
-    held = gather_blocks(n_grp, n_tile, cap, blocks, places, *beads)
-    selfs = self_terms(blocks, *beads)
+    pairs = tile_couplings.transpose(0, 2, 1)
+    held, early = gather_blocks(n_grp, n_tile, cap, blocks, places, *beads)
     terms = pair_terms(n_tile, cap, pairs, processor_coupling_tally, held)
-    got = return_terms(n_grp, n_tile, terms)
-    return total_terms(n_tile, cap, blocks, places, got, selfs)
+    got, late = return_terms(n_grp, n_tile, blocks, terms, beads)
+    return total_terms(n_tile, cap, blocks, places, got, early, late)
 
 
 def solution(mesh):

time: 205 us -> 135 us (0.66)
  Pallas kernels: 193 us -> 131 us
  local copies, waits for them, and re-layouts: 8.79 us -> 1.29 us
    pallas_call x2 -> x1, Pallas kernels: 90.4 us -> 28.1 us  [return_terms(): pl.pallas_call(functools.partial(return_kernel, n_grp, n_tile, blocks), o...]
    unnamed x28 -> x1, local copies, waits for them, and re-layouts: 7.82 us -> 1.29 us
    pallas_call x1, Pallas kernels: 77 us -> 74.3 us  [pair_terms(): pl.pallas_call(functools.partial(pair_kernel, n_tile, cap), out_shape=jax...]
    pallas_call x1, Pallas kernels: 23.7 us -> 26 us  [gather_blocks(): pl.pallas_call(functools.partial(gather_kernel, n_grp, n_tile, cap, block...]
where the time goes in v2:
time: 135 us; the launch traced here: 133 us
  Pallas kernels  131 us (97%)
    pallas_call x1, Pallas kernels, pair_terms(): pl.pallas_call(functools.partial(pair_kernel, n_tile, cap), out_shape=jax...  74.3 us
    pallas_call x1, Pallas kernels, return_terms(): pl.pallas_call(functools.partial(return_kernel, n_grp, n_tile, blocks), o...  28.1 us
    pallas_call x1, Pallas kernels, gather_blocks(): pl.pallas_call(functools.partial(gather_kernel, n_grp, n_tile, cap, block...  26 us
    pallas_call x1, Pallas kernels, total_terms(): pl.pallas_call(functools.partial(total_kernel, n_tile, cap, blocks), out_...  2.76 us

profile of v2, /device:TPU:99, one launch (start us, length us, event | category | flops | bytes accessed | tf_op | source)
XLA Modules:
  0.0 133.1 jit_solution(12176780097893472485)
XLA Ops:
  0.7 1.3 copy.11
  1.9 26.0 %gather_blocks.1 = (f32[32,112,128]{2,1,0:T(8,128)}, f32[64,4,128]{2,1,0:T(4,128)}) custom-call(s32[1,12,16]{2,1,0:T(8,128)} %bitcast.13, f32[3,16384]{1,0:T(4,128)} %coords_hbm.3, f32[3,16384]{1,0:T(4,128)} %speeds_hbm.3, f32[128,128]{1,0:T(8,128)} %bitcast.7, f32[128,128]{1,0:T(8,128)} %bitcast.9, s32[128,128]{1,0:T(8,128)} %bitcast.11), custom_call_target="tpu_custom_call" | custom-call | tf_op jit(solution)/shard_map/gather_blocks/pallas_call | solution.py:295
  27.9 74.3 %pair_terms.1.terms_ref = f32[32,48,128]{2,1,0:T(8,128)} custom-call(s32[1,2,1024]{2,1,0:T(2,128)} %bitcast.15, s32[1]{0:T(128)S(6)} %copy.12.live_ref, f32[32,112,128]{2,1,0:T(8,128)} %get-tuple-element.9.held_hbm), custom_call_target="tpu_custom_call" | custom-call | tf_op jit(solution)/shard_map/pair_terms/pallas_call | solution.py:455
  102.2 28.1 %return_terms.1 = (f32[32,48,128]{2,1,0:T(8,128)}, f32[64,4,128]{2,1,0:T(4,128)}) custom-call(f32[32,48,128]{2,1,0:T(8,128)} %pair_terms.1.terms_ref, f32[3,16384]{1,0:T(4,128)} %coords_hbm.3, f32[3,16384]{1,0:T(4,128)} %speeds_hbm.3, f32[128,128]{1,0:T(8,128)} %bitcast.8, f32[128,128]{1,0:T(8,128)} %bitcast.10, s32[128,128]{1,0:T(8,128)} %bitcast.12), custom_call_target="tpu_custom_call" | custom-call | tf_op jit(solution)/shard_map/return_terms/pallas_call | solution.py:545
  130.4 2.8 %total_terms.1 = f32[4,16384]{1,0:T(4,128)} custom-call(s32[1,12,16]{2,1,0:T(8,128)} %bitcast.14, f32[32,48,128]{2,1,0:T(8,128)} %get-tuple-element.10.got_ref, f32[64,4,128]{2,1,0:T(4,128)} %get-tuple-element.11.early_ref, f32[64,4,128]{2,1,0:T(4,128)} %get-tuple-element.12.late_ref), custom_call_target="tpu_custom_call" | custom-call | tf_op jit(solution)/shard_map/total_terms/pallas_call | solution.py:587

commit v3 on v2

--- a/solution.py
+++ b/solution.py
@@ -141,19 +141,16 @@
     return high, (value - high.astype(F32)).astype(BF16)
 
 
-SELF_GANG = 4
-
-
 def result_rows(base, sums, heat):
     moved = sums[0:3] + sums[8:11] + sums[11:14]
     force = FORCE_UNIT * (base[0:3] * sums[14:15] - moved)
     return jnp.concatenate([force, HEAT_UNIT * heat], 0)
 
 
-def self_blocks(first, beads, out_ref, at):
+def self_blocks(first, count, beads, out_ref):
     coords_ref, speeds_ref, temp_ref, strength_ref, keys_ref = beads
     raws, seeds, factors = [], [], []
-    for n in range(SELF_GANG):
+    for n in range(count):
         b = first + n
         lanes = pl.ds(pl.multiple_of(b * 128, 128), 128)
         raws.append(
@@ -168,21 +165,21 @@
     wide, slim = wide_rows(terms)
     tall, weigh = tall_rows(terms), weigh_rows(terms)
     stacks = [
-        jnp.concatenate([tall[n], jnp.broadcast_to(seeds[n].astype(F32), (64, 128))], 0).T for n in range(SELF_GANG)
+        jnp.concatenate([tall[n], jnp.broadcast_to(seeds[n].astype(F32), (64, 128))], 0).T for n in range(count)
     ]
-    both = [products(stacks[n][:, :K_WIDE].astype(BF16), wide[n], slim[n]) for n in range(SELF_GANG)]
+    both = [products(stacks[n][:, :K_WIDE].astype(BF16), wide[n], slim[n]) for n in range(count)]
     halved, heats = [], []
-    for n in range(SELF_GANG):
+    for n in range(count):
         mine = jnp.broadcast_to(stacks[n][:, K_WIDE : K_WIDE + 1].astype(I32), (128, 128))
         gain, _, heat = finish(both[n], mine, factors[n])
         halved.append(jnp.concatenate(halves(gain), 0))
         heats.append(jnp.sum(heat, 0, keepdims=True))
-    for n in range(0, SELF_GANG, 2):
+    for n in range(0, count, 2):
         left = jnp.concatenate([jnp.concatenate([weigh[m], weigh[m]], 1) for m in (n, n + 1)], 0)
         sums = jnp.dot(left, jnp.concatenate(halved[n : n + 2], 1), preferred_element_type=F32)
         for m in (0, 1):
             mine = sums[16 * m : 16 * m + 16, 128 * m : 128 * m + 128]
-            out_ref[at + n + m] = result_rows(terms[1][n + m], mine, heats[n + m])
+            out_ref[first + n + m] = result_rows(terms[1][n + m], mine, heats[n + m])
 
 
 def gather_kernel(
@@ -253,17 +250,17 @@
     home.start()
     upward(t, box).start()
 
+    share = blocks // n_tile
+
     def take(step, carry):
         owner = lax.rem(t + n_tile - step, n_tile)
         incoming(owner).wait_recv()
         upward(owner, held_ref).start()
-        some = (step - 1) * SELF_GANG
-        self_blocks(some, beads, self_ref, some)
+        self_blocks((step - 1) * share, share, beads, self_ref)
         return carry
 
     lax.fori_loop(1, n_tile, take, 0)
-    last = (n_tile - 1) * SELF_GANG
-    self_blocks(last, beads, self_ref, last)
+    self_blocks((n_tile - 1) * share, share, beads, self_ref)
     home.wait()
 
     def finish(owner, carry):
@@ -296,7 +293,7 @@
         functools.partial(gather_kernel, n_grp, n_tile, cap, blocks),
         out_shape=[
             jax.ShapeDtypeStruct((2 * n_tile, rows, 128), F32),
-            jax.ShapeDtypeStruct((n_tile * SELF_GANG, 4, 128), F32),
+            jax.ShapeDtypeStruct((blocks, 4, 128), F32),
         ],
         in_specs=[pl.BlockSpec(memory_space=pltpu.SMEM)] + [hbm] * 5,
         out_specs=[hbm, vmem],
@@ -310,15 +307,16 @@
     )(places, coords, speeds, temp, strength, keys)
 
 
-GANG = 16
+GANG = 64
 AHEAD = 0
 LAG = 6
 LAG_AT = 0
+SETTLE_AT = 9
 
 
 def pair_kernel(
     n_tile, cap, pairs_ref, live_ref, held_hbm, out_ref,
-    held_ref, held_sems, tall_s, wide_s, slim_s, weigh_s, seeds_s, factor_s, acc, heat_acc, *gains,
+    held_ref, held_sems, tall_s, wide_s, slim_s, weigh_s, seeds_s, factor_s, acc, column_s, *gains,
 ):
     slots = n_tile * cap
 
@@ -350,7 +348,6 @@
                     stack = jnp.concatenate([tall[n], mine], 0).T
                     tall_s[slot + n] = stack[:, :K_WIDE].astype(BF16)
                     seeds_s[slot + n] = jnp.broadcast_to(stack[:, K_WIDE : K_WIDE + 1].astype(I32), (128, 128))
-                    heat_acc[slot + n] = jnp.zeros((128, 128), F32)
 
     def near_step(owner, carry):
         prepare(owner, owner * cap, True)
@@ -366,9 +363,10 @@
     lax.fori_loop(0, n_tile, far_step, 0)
 
     live = live_ref[0]
-
-    def gang(step, carry):
-        made = {}
+    column_s[...] = jnp.zeros((128, 128), F32)
+
+    def gang(step, carry, whole=True):
+        made, columns = {}, []
 
         def place(u):
             k = step * GANG + u
@@ -382,7 +380,7 @@
         def evaluate(u):
             p, q, dead = place(u)
             gain, heat_p, heat_q = finish(made.pop(u), seeds_s[p], factor_s[q])
-            heat_acc[jnp.where(dead, slots, p)] += heat_p
+            columns.append(jnp.sum(heat_p, 1, keepdims=True))
             acc[jnp.where(dead, 2 * slots, q), 16:24] += jnp.sum(heat_q.reshape(16, 8, 128), 0)
             gains[u % GANG][0:128], gains[u % GANG][128:256] = halves(gain)
 
@@ -404,6 +402,18 @@
                 acc[jnp.where(dead, 2 * slots, p), 0:16] += on_p[rows, lanes]
                 acc[jnp.where(dead, 2 * slots, q), 0:16] += on_q[rows, lanes]
 
+        def settle():
+            rows = column_s[...].T
+            for u in range(GANG):
+                p, _, dead = place(u - GANG)
+                acc[jnp.where(dead, 2 * slots, p), 16:17] += rows[u : u + 1]
+
+        if not whole:
+            for u in range(0, LAG, 2):
+                reduce(u - LAG)
+            settle()
+            return carry
+
         for u in range(-AHEAD, GANG):
             if 0 <= u + AHEAD < GANG:
                 multiply(u + AHEAD)
@@ -411,27 +421,22 @@
                 evaluate(u)
                 if u % 2 == LAG_AT:
                     reduce(u - LAG_AT - LAG)
-        return carry
-
-    lax.fori_loop(0, lax.div(live + LAG + GANG - 1, GANG), gang, 0)
-
-    ones = jnp.ones((16, 256), BF16)
+                if u == SETTLE_AT:
+                    settle()
+        column_s[:, 0:GANG] = jnp.concatenate(columns, 1)
+        return carry
+
+    gangs = lax.div(live + GANG - 1, GANG)
+    lax.fori_loop(0, gangs, gang, 0)
+    gang(gangs, 0, False)
 
     def near_out(owner, carry):
         boxed = held_ref.at[owner]
-        for c in range(0, cap, 2):
-            rows = []
-            for n in (0, 1):
-                rows.append(jnp.concatenate(halves(heat_acc[owner * cap + c + n]), 1))
-            heats = lax.dot_general(
-                ones, jnp.concatenate(rows, 0), (((1,), (1,)), ((), ())), preferred_element_type=F32
-            )
-            for n in (0, 1):
-                slot = owner * cap + c + n
-                sums = acc[slot]
-                heat = jnp.sum(sums[16:24], 0, keepdims=True) + heats[0:1, 128 * n : 128 * n + 128]
-                base = boxed[8 * (c + n) : 8 * (c + n) + 8] - MIDDLE
-                out_ref[owner, 4 * (c + n) : 4 * (c + n) + 4] = result_rows(base, sums, heat)
+        for c in range(cap):
+            sums = acc[owner * cap + c]
+            heat = jnp.sum(sums[16:24], 0, keepdims=True)
+            base = boxed[8 * c : 8 * c + 8] - MIDDLE
+            out_ref[owner, 4 * c : 4 * c + 4] = result_rows(base, sums, heat)
         return carry
 
     def far_out(owner, carry):
@@ -467,7 +472,7 @@
             pltpu.VMEM((slots, 128, 128), I32),
             pltpu.VMEM((2 * slots, 1, 128), I32),
             pltpu.VMEM((2 * slots + 1, 24, 128), F32),
-            pltpu.VMEM((slots + 1, 128, 128), F32),
+            pltpu.VMEM((128, 128), F32),
             *[pltpu.VMEM((256, 128), BF16)] * GANG,
         ],
         compiler_params=pltpu.CompilerParams(vmem_limit_bytes=63 * MIB),
@@ -476,13 +481,8 @@
 
 
 def return_kernel(
-    n_grp, n_tile, blocks, terms_ref, coords_hbm, speeds_hbm, temp_hbm, strength_hbm, keys_hbm,
-    got_ref, self_ref, send_sems, recv_sems, home_sem, bead_sems, *beads,
+    n_grp, n_tile, terms_ref, got_ref, send_sems, recv_sems, home_sem,
 ):
-    sources = (coords_hbm, speeds_hbm, temp_hbm, strength_hbm, keys_hbm)
-    loads = [pltpu.make_async_copy(source, beads[n], bead_sems.at[n]) for n, source in enumerate(sources)]
-    for load in loads:
-        load.start()
     g, t = lax.axis_index("grp"), lax.axis_index("tile")
     above, below = lax.rem(g + 1, n_grp), lax.rem(g + n_grp - 1, n_grp)
     barrier = pltpu.get_barrier_semaphore()
@@ -515,15 +515,6 @@
     lax.fori_loop(1, n_tile, start, 0)
     home = pltpu.make_async_copy(terms_ref.at[t], got_ref.at[t], home_sem)
     home.start()
-    for load in loads:
-        load.wait()
-    done = n_tile * SELF_GANG
-
-    def selfs(step, carry):
-        self_blocks(done + step * SELF_GANG, beads, self_ref, step * SELF_GANG)
-        return carry
-
-    lax.fori_loop(0, (blocks - done) // SELF_GANG, selfs, 0)
     home.wait()
     far(t, t).wait()
 
@@ -538,31 +529,23 @@
     lax.fori_loop(1, n_tile, finish, 0)
 
 
-def return_terms(n_grp, n_tile, blocks, terms, beads):
+def return_terms(n_grp, n_tile, terms):
     vmem = pl.BlockSpec(memory_space=pltpu.VMEM)
     hbm = pl.BlockSpec(memory_space=pltpu.HBM)
     sems = pltpu.SemaphoreType.DMA((2 * n_tile,))
     return pl.pallas_call(
-        functools.partial(return_kernel, n_grp, n_tile, blocks),
-        out_shape=[
-            jax.ShapeDtypeStruct(terms.shape, F32),
-            jax.ShapeDtypeStruct((blocks - n_tile * SELF_GANG, 4, 128), F32),
-        ],
-        in_specs=[hbm] * 6,
-        out_specs=[vmem, vmem],
-        scratch_shapes=[
-            sems, sems, pltpu.SemaphoreType.DMA, pltpu.SemaphoreType.DMA((5,)),
-            *bead_buffers(blocks),
-        ],
+        functools.partial(return_kernel, n_grp, n_tile),
+        out_shape=jax.ShapeDtypeStruct(terms.shape, F32),
+        in_specs=[hbm],
+        out_specs=vmem,
+        scratch_shapes=[sems, sems, pltpu.SemaphoreType.DMA],
         compiler_params=pltpu.CompilerParams(collective_id=1, has_side_effects=True, vmem_limit_bytes=63 * MIB),
         name="return_terms",
-    )(terms, *beads)
-
-
-def total_kernel(n_tile, cap, blocks, places_ref, got_ref, early_ref, late_ref, out_ref, acc):
-    early = early_ref.shape[0]
-    acc[0:early] = early_ref[...]
-    acc[early:blocks] = late_ref[...]
+    )(terms)
+
+
+def total_kernel(n_tile, cap, blocks, places_ref, got_ref, self_ref, out_ref, acc):
+    acc[...] = self_ref[...]
 
     def add(worker, carry):
         for c in range(cap):
@@ -580,19 +563,19 @@
     lax.fori_loop(0, blocks, put, 0, unroll=8)
 
 
-def total_terms(n_tile, cap, blocks, places, got, early, late):
+def total_terms(n_tile, cap, blocks, places, got, selfs):
     smem = pl.BlockSpec(memory_space=pltpu.SMEM)
     vmem = pl.BlockSpec(memory_space=pltpu.VMEM)
     hbm = pl.BlockSpec(memory_space=pltpu.HBM)
     return pl.pallas_call(
         functools.partial(total_kernel, n_tile, cap, blocks),
         out_shape=jax.ShapeDtypeStruct((4, blocks * 128), F32),
-        in_specs=[smem, vmem, vmem, vmem],
+        in_specs=[smem, vmem, vmem],
         out_specs=vmem,
         scratch_shapes=[pltpu.VMEM((blocks, 4, 128), F32)],
         compiler_params=pltpu.CompilerParams(vmem_limit_bytes=63 * MIB),
         name="total_terms",
-    )(places, got, early, late)
+    )(places, got, selfs)
 
 
 def per_device(
@@ -617,10 +600,10 @@
         noise_keys.reshape(blocks, 128),
     )
     pairs = tile_couplings.transpose(0, 2, 1)
-    held, early = gather_blocks(n_grp, n_tile, cap, blocks, places, *beads)
+    held, selfs = gather_blocks(n_grp, n_tile, cap, blocks, places, *beads)
     terms = pair_terms(n_tile, cap, pairs, processor_coupling_tally, held)
-    got, late = return_terms(n_grp, n_tile, blocks, terms, beads)
-    return total_terms(n_tile, cap, blocks, places, got, early, late)
+    got = return_terms(n_grp, n_tile, terms)
+    return total_terms(n_tile, cap, blocks, places, got, selfs)
 
 
 def solution(mesh):

time: 135 us -> 129 us (0.956); the launches traced: 133 us -> 129 us
  Pallas kernels: 131 us -> 127 us
    pallas_call x1, Pallas kernels: 28.1 us -> 22.4 us  [return_terms(): pl.pallas_call(functools.partial(return_kernel, n_grp, n_tile), out_shape...]
where the time goes in v3:
time: 129 us
  Pallas kernels  127 us (98%)
    pallas_call x1, Pallas kernels, pair_terms(): pl.pallas_call(functools.partial(pair_kernel, n_tile, cap), out_shape=jax...  74.5 us
    pallas_call x1, Pallas kernels, gather_blocks(): pl.pallas_call(functools.partial(gather_kernel, n_grp, n_tile, cap, block...  27.2 us
    pallas_call x1, Pallas kernels, return_terms(): pl.pallas_call(functools.partial(return_kernel, n_grp, n_tile), out_shape...  22.4 us
    pallas_call x1, Pallas kernels, total_terms(): pl.pallas_call(functools.partial(total_kernel, n_tile, cap, blocks), out_...  2.74 us

profile of v3, /device:TPU:99, one launch (start us, length us, event | category | flops | bytes accessed | tf_op | source)
XLA Modules:
  0.0 128.8 jit_solution(12058391121341973317)
XLA Ops:
  0.7 1.3 copy.11
  1.9 27.2 %gather_blocks.1 = (f32[32,112,128]{2,1,0:T(8,128)}, f32[128,4,128]{2,1,0:T(4,128)}) custom-call(s32[1,12,16]{2,1,0:T(8,128)} %bitcast.7, f32[3,16384]{1,0:T(4,128)} %coords_hbm.1, f32[3,16384]{1,0:T(4,128)} %speeds_hbm.1, f32[128,128]{1,0:T(8,128)} %bitcast.9, f32[128,128]{1,0:T(8,128)} %bitcast.10, s32[128,128]{1,0:T(8,128)} %bitcast.11), custom_call_target="tpu_custom_call" | custom-call | tf_op jit(solution)/shard_map/gather_blocks/pallas_call | solution.py:292
  29.2 74.5 %pair_terms.1.terms_ref = f32[32,48,128]{2,1,0:T(8,128)} custom-call(s32[1,2,1024]{2,1,0:T(2,128)} %bitcast.12, s32[1]{0:T(128)S(6)} %copy.12.live_ref, f32[32,112,128]{2,1,0:T(8,128)} %get-tuple-element.7.held_hbm), custom_call_target="tpu_custom_call" | custom-call | tf_op jit(solution)/shard_map/pair_terms/pallas_call | solution.py:460
  103.7 22.4 %return_terms.1.got_ref = f32[32,48,128]{2,1,0:T(8,128)} custom-call(f32[32,48,128]{2,1,0:T(8,128)} %pair_terms.1.terms_ref), custom_call_target="tpu_custom_call" | custom-call | tf_op jit(solution)/shard_map/return_terms/pallas_call | solution.py:536
  126.1 2.7 %total_terms.1 = f32[4,16384]{1,0:T(4,128)} custom-call(s32[1,12,16]{2,1,0:T(8,128)} %bitcast.8, f32[32,48,128]{2,1,0:T(8,128)} %return_terms.1.got_ref, f32[128,4,128]{2,1,0:T(4,128)} %get-tuple-element.8.self_ref), custom_call_target="tpu_custom_call" | custom-call | tf_op jit(solution)/shard_map/total_terms/pallas_call | solution.py:570

commit v4 on v3

--- a/solution.py
+++ b/solution.py
@@ -214,7 +214,7 @@
 
     def fill(worker):
         for c in range(cap):
-            place = places_ref[0, c, worker]
+            place = places_ref[c, 0, worker]
             box[worker, 8 * c : 8 * c + 8] = own[place, 0:8]
             box[worker, 8 * cap + c : 8 * cap + c + 1] = own[place, 8:9]
 
@@ -256,11 +256,20 @@
         owner = lax.rem(t + n_tile - step, n_tile)
         incoming(owner).wait_recv()
         upward(owner, held_ref).start()
-        self_blocks((step - 1) * share, share, beads, self_ref)
-        return carry
-
-    lax.fori_loop(1, n_tile, take, 0)
-    self_blocks((n_tile - 1) * share, share, beads, self_ref)
+        return carry
+
+    def share_of(part, carry):
+        self_blocks(part * share, share, beads, self_ref)
+        return carry
+
+    def take_beside(step, carry):
+        take(step, carry)
+        return share_of(EARLY + step - 1, carry)
+
+    lax.fori_loop(0, EARLY, share_of, 0)
+    lax.fori_loop(1, BESIDE + 1, take_beside, 0)
+    lax.fori_loop(BESIDE + 1, n_tile, take, 0)
+    lax.fori_loop(EARLY + BESIDE, n_tile, share_of, 0)
     home.wait()
 
     def finish(owner, carry):
@@ -308,6 +317,8 @@
 
 
 GANG = 64
+EARLY = 3
+BESIDE = 6
 AHEAD = 0
 LAG = 6
 LAG_AT = 0
@@ -344,10 +355,9 @@
             if with_tall:
                 tall = tall_rows(terms)
                 for n in range(4):
-                    mine = jnp.broadcast_to(seed[c + n : c + n + 1].astype(F32), (64, 128))
-                    stack = jnp.concatenate([tall[n], mine], 0).T
-                    tall_s[slot + n] = stack[:, :K_WIDE].astype(BF16)
-                    seeds_s[slot + n] = jnp.broadcast_to(stack[:, K_WIDE : K_WIDE + 1].astype(I32), (128, 128))
+                    mine = jnp.broadcast_to(seed[c + n : c + n + 1], (128, 128))
+                    tall_s[slot + n] = tall[n].astype(BF16).T
+                    seeds_s[slot + n] = mine.T
 
     def near_step(owner, carry):
         prepare(owner, owner * cap, True)
@@ -549,7 +559,7 @@
 
     def add(worker, carry):
         for c in range(cap):
-            place = places_ref[0, c, worker]
+            place = places_ref[c, 0, worker]
             rows = slice(4 * c, 4 * c + 4)
             acc[place] += got_ref[worker, rows] + got_ref[n_tile + worker, rows]
         return carry
@@ -591,7 +601,7 @@
     n_grp, n_tile = lax.axis_size("grp"), lax.axis_size("tile")
     blocks = molecule_coords.shape[1] // 128
     cap = exported_tile_places.shape[2]
-    places = exported_tile_places.transpose(0, 2, 1)
+    places = exported_tile_places.transpose(2, 0, 1)
     beads = (
         molecule_coords,
         molecule_speeds,

time: 129 us -> 125 us (0.969); the launches traced: 129 us -> 123 us
  Pallas kernels: 127 us -> 122 us
    pallas_call x1, Pallas kernels: 74.5 us -> 51.8 us  [pair_terms(): pl.pallas_call(functools.partial(pair_kernel, n_tile, cap), out_shape=jax...]
    pallas_call x1, Pallas kernels: 22.4 us -> 42.6 us  [return_terms(): pl.pallas_call(functools.partial(return_kernel, n_grp, n_tile), out_shape...]
    pallas_call x1, Pallas kernels: 27.2 us -> 25.1 us  [gather_blocks(): pl.pallas_call(functools.partial(gather_kernel, n_grp, n_tile, cap, block...]
where the time goes in v4:
time: 125 us; the launch traced here: 123 us
  Pallas kernels  122 us (98%)
    pallas_call x1, Pallas kernels, pair_terms(): pl.pallas_call(functools.partial(pair_kernel, n_tile, cap), out_shape=jax...  51.8 us
    pallas_call x1, Pallas kernels, return_terms(): pl.pallas_call(functools.partial(return_kernel, n_grp, n_tile), out_shape...  42.6 us
    pallas_call x1, Pallas kernels, gather_blocks(): pl.pallas_call(functools.partial(gather_kernel, n_grp, n_tile, cap, block...  25.1 us
    pallas_call x1, Pallas kernels, total_terms(): pl.pallas_call(functools.partial(total_kernel, n_tile, cap, blocks), out_...  2.74 us

profile of v4, /device:TPU:99, one launch (start us, length us, event | category | flops | bytes accessed | tf_op | source)
XLA Modules:
  0.0 122.8 jit_solution(17853485835992685672)
XLA Ops:
  0.7 25.1 %gather_blocks.1 = (f32[32,112,128]{2,1,0:T(8,128)}, f32[128,4,128]{2,1,0:T(4,128)}) custom-call(s32[12,1,16]{2,1,0:T(1,128)} %bitcast.8, f32[3,16384]{1,0:T(4,128)} %coords_hbm.1, f32[3,16384]{1,0:T(4,128)} %speeds_hbm.1, f32[128,128]{1,0:T(8,128)} %bitcast.5, f32[128,128]{1,0:T(8,128)} %bitcast.6, s32[128,128]{1,0:T(8,128)} %bitcast.7), custom_call_target="tpu_custom_call" | custom-call | tf_op jit(solution)/shard_map/gather_blocks/pallas_call | solution.py:301
  25.7 51.8 %pair_terms.1.terms_ref = f32[32,48,128]{2,1,0:T(8,128)} custom-call(s32[1,2,1024]{2,1,0:T(2,128)} %bitcast.10, s32[1]{0:T(128)S(6)} %copy.9.live_ref, f32[32,112,128]{2,1,0:T(8,128)} %get-tuple-element.7.held_hbm), custom_call_target="tpu_custom_call" | custom-call | tf_op jit(solution)/shard_map/pair_terms/pallas_call | solution.py:470
  77.5 42.6 %return_terms.1.got_ref = f32[32,48,128]{2,1,0:T(8,128)} custom-call(f32[32,48,128]{2,1,0:T(8,128)} %pair_terms.1.terms_ref), custom_call_target="tpu_custom_call" | custom-call | tf_op jit(solution)/shard_map/return_terms/pallas_call | solution.py:546
  120.1 2.7 %total_terms.1 = f32[4,16384]{1,0:T(4,128)} custom-call(s32[12,1,16]{2,1,0:T(1,128)} %bitcast.9, f32[32,48,128]{2,1,0:T(8,128)} %return_terms.1.got_ref, f32[128,4,128]{2,1,0:T(4,128)} %get-tuple-element.8.self_ref), custom_call_target="tpu_custom_call" | custom-call | tf_op jit(solution)/shard_map/total_terms/pallas_call | solution.py:580
